TPU v7x, 32 devices: a whole 2x2x4 slice. The times are simulated.
32 devices in a mesh: img: 8 (over z, x), lat: 4 (over y, core).
Axes of the slice: x: 2, y: 2, z: 4, core: 2. Of those that a mesh axis runs over, the one named last changes fastest.
Arguments:
- media: bfloat16 [98304, 1024], P(('img', 'lat')), may hold values from -6 to 6
- latents: float32 [192, 64, 1024], P('img', 'lat'), may hold values from -6 to 6
- counts: int32 [8, 24], P('img'), may hold values from 1 to 6, 48 in all within a row
- cotangent: bfloat16 [192, 64, 1024], P('img', 'lat'), may hold values from -6 to 6
- attend_weight: float32 [1024, 1536], P(('img', 'lat')), may hold values from -0.1875 to 0.1875
- output_weight: float32 [512, 1024], P(('img', 'lat')), may hold values from -4 to 4
- expand_weight: float32 [1024, 4096], P(('img', 'lat')), may hold values from -0.1875 to 0.1875
- shrink_weight: float32 [4096, 1024], P(('img', 'lat')), may hold values from -0.09375 to 0.09375
- layer_gains: float32 [1024, 3], P(('img', 'lat')), may hold values from 0.24 to 3.6
- layer_biases: float32 [1024, 3], P(('img', 'lat')), may hold values from -1.2 to 1.2
- attend_momentum: float32 [1024, 1536], P(('img', 'lat')), may hold values from -0.00021362305 to 0.00021362305
- output_momentum: float32 [512, 1024], P(('img', 'lat')), may hold values from -0.00021362305 to 0.00021362305
- expand_momentum: float32 [1024, 4096], P(('img', 'lat')), may hold values from -0.00021362305 to 0.00021362305
- shrink_momentum: float32 [4096, 1024], P(('img', 'lat')), may hold values from -0.00021362305 to 0.00021362305
- gains_momentum: float32 [1024, 3], P(('img', 'lat')), may hold values from -0.0008544922 to 0.0008544922
- biases_momentum: float32 [1024, 3], P(('img', 'lat')), may hold values from -0.0008544922 to 0.0008544922
- attend_average: float32 [1024, 1536], P(('img', 'lat')), may hold values from -0.1875 to 0.1875
- output_average: float32 [512, 1024], P(('img', 'lat')), may hold values from -4 to 4
- expand_average: float32 [1024, 4096], P(('img', 'lat')), may hold values from -0.1875 to 0.1875
- shrink_average: float32 [4096, 1024], P(('img', 'lat')), may hold values from -0.09375 to 0.09375
- gains_average: float32 [1024, 3], P(('img', 'lat')), may hold values from 0.5 to 1.5
- biases_average: float32 [1024, 3], P(('img', 'lat')), may hold values from -1.2 to 1.2
Outputs:
- latents_out: float32 [192, 64, 1024], P('img', 'lat')
- media_grad: bfloat16 [98304, 1024], P(('img', 'lat'))
- latents_grad: float32 [192, 64, 1024], P('img', 'lat')
- grad_norm: float32 [], replicated
- attend_master: float32 [1024, 1536], P(('img', 'lat'))
- output_master: float32 [512, 1024], P(('img', 'lat'))
- expand_master: float32 [1024, 4096], P(('img', 'lat'))
- shrink_master: float32 [4096, 1024], P(('img', 'lat'))
- gains_master: float32 [1024, 3], P(('img', 'lat'))
- biases_master: float32 [1024, 3], P(('img', 'lat'))
- attend_buffer: float32 [1024, 1536], P(('img', 'lat'))
- output_buffer: float32 [512, 1024], P(('img', 'lat'))
- expand_buffer: float32 [1024, 4096], P(('img', 'lat'))
- shrink_buffer: float32 [4096, 1024], P(('img', 'lat'))
- gains_buffer: float32 [1024, 3], P(('img', 'lat'))
- biases_buffer: float32 [1024, 3], P(('img', 'lat'))
- attend_smoothed: float32 [1024, 1536], P(('img', 'lat'))
- output_smoothed: float32 [512, 1024], P(('img', 'lat'))
- expand_smoothed: float32 [1024, 4096], P(('img', 'lat'))
- shrink_smoothed: float32 [4096, 1024], P(('img', 'lat'))
- gains_smoothed: float32 [1024, 3], P(('img', 'lat'))
- biases_smoothed: float32 [1024, 3], P(('img', 'lat'))
Inputs may be any that keep to these rules, and one draw needn't show every extreme that they name: Each row of counts holds 24 whole numbers that sum to 48; the largest of a row is exactly 6.
All inputs are finite; a program needn't handle non-finite values.
Results may differ from a plain program's by a relative error of at most 0.017.
The roundings to bfloat16 on the way count: a program that leaves them out, or rounds other values in their place, can miss the bound.
Values may be sent and summed in bfloat16 or wider, within the bound.
A program may use at most 256 MiB of HBM per device.

v0:
```python
import functools
import math

import jax
import jax.numpy as jnp
from jax import lax
from jax.experimental import pallas as pl
from jax.experimental.pallas import tpu as pltpu
from jax.sharding import PartitionSpec as P

HEADS = 8
HDIM = 64
PATCH_IMG = 256
GROUP = 4
TOGETHER = 2
EPS = 1e-05
MOMENTUM = 0.9
DECAY = 0.0001
AVERAGING = 0.6
CLIP_NORM = 1.0
RATE_SCALES = (1.0, 100.0, 1.0, 1.0, 15.0, 1.0)
AXES = ("img", "lat")
LANES = 128
BLOCKS = 32
SCALE = HDIM ** (-0.5)
MASKED = -1e30
F32 = jnp.float32
BF16 = jnp.bfloat16
MESH = pl.DeviceIdType.MESH
START_PLAN = ("b0", "a1", "c0", "b1", "a2", "c1", "b2", "a3", "c2", "b3", "c3")
HEAD_FLIPS = (0,)
BACK_FLIPS = ()
HEAD_PLAN = ((2, ('ea1', 'ez2', 'eb0')), (9, ('ez3',)), (12, ('eb1', 'ea2')), (19, ('ec0', 'eb2', 'ea3', 'sz1')), (24, ('ec1', 'eb3', 'sa0')), (26, ('ec2', 'ec3', 'sa1', 'sz2', 'sb0')))
HEAD_LATE = (
    ("sz3",),
    ("sc0", "sb1", "sa2"),
    (),
    (),
    ("sc1", "sb2", "sa3"),
    ("sc2", "sb3"),
    ("sc3",),
)
BACK_PLAN = ((0, ('a0',)), (1, ('a1',)), (3, ('b0',)), (4, ('a2',)), (7, ('c0', 'b1')), (8, ('a3',)), (11, ('c1', 'b2')), (13, ('c2', 'b3')), (13, ('c3',)))
NORM_PLAN = ("a0", "a1", "b0", "a2", "b1", "c0", "a3", "b2", "c1", "b3", "c2", "c3")
VMEM_LIMIT = 60 * 1024 * 1024


def mm(a, b):
    return jnp.dot(a, b, preferred_element_type=F32)


def mm_tn(a, b):
    return lax.dot_general(a, b, (((0,), (0,)), ((), ())), preferred_element_type=F32)


def mm_nt(a, b):
    return lax.dot_general(a, b, (((1,), (1,)), ((), ())), preferred_element_type=F32)


def any_spec():
    return pl.BlockSpec(memory_space=pl.ANY)


def vmem_spec():
    return pl.BlockSpec(memory_space=pltpu.VMEM)


def params(**more):
    return pltpu.CompilerParams(vmem_limit_bytes=VMEM_LIMIT, **more)


def place():
    img = lax.axis_index("img")
    lat = lax.axis_index("lat")
    return img // 2, img % 2, lat // 2, lat % 2


def flat(a, b, e, c):
    return ((a * 2 + b) * 2 + e) * 2 + c


def device(a, b, e, c):
    return (a * 2 + b, e * 2 + c)


def neighbours(a, b, e, c, colour):
    one = (a, (b + 1 - colour) % 2, (e + colour) % 2, c)
    two = (a, (b + colour) % 2, (e + 1 - colour) % 2, c)
    return [(a, b, e, c), one, two, (a, 1 - b, 1 - e, c)]


def z_order(depth):
    order = [0]
    for k in range(1, depth // 2 + 1):
        order.append(k)
        if depth - k != k:
            order.append(depth - k)
    return order


def greet(depth, a, b, e, c):
    barrier = pltpu.get_barrier_semaphore()
    friends = [device((a + k) % depth, b, e, c) for k in range(1, depth)]
    friends += [device(a, 1 - b, e, c), device(a, b, 1 - e, c), device(a, b, e, 1 - c)]
    for friend in friends:
        pl.semaphore_signal(barrier, inc=1, device_id=friend, device_id_type=MESH)
    pl.semaphore_wait(barrier, len(friends))


def add_into(target, first, second, chunk):
    @pl.loop(0, target.shape[1] // chunk)
    def _(step):
        part = pl.ds(pl.multiple_of(step * chunk, chunk), chunk)
        target[:, part] = first[:, part] + second[:, part]


def normalise(values):
    center = values - jnp.mean(values, axis=-1, keepdims=True)
    spread = jnp.mean(center * center, axis=-1, keepdims=True)
    scale = lax.rsqrt(spread + EPS)
    return center * scale, scale


def norm_back(grad, hat, scale, gain):
    inner = grad * gain
    first = jnp.mean(inner, axis=-1, keepdims=True)
    second = jnp.mean(inner * hat, axis=-1, keepdims=True)
    return scale * (inner - first - hat * second)


def media_kernel(m_ref, gb_ref, wk_ref, wv_ref, k_ref, v_ref):
    hat, _ = normalise(m_ref[...].astype(F32))
    normed = (hat * gb_ref[0:1, :] + gb_ref[3:4, :]).astype(BF16)
    k_ref[...] = mm(normed, wk_ref[...]).astype(BF16)
    v_ref[...] = mm(normed, wv_ref[...]).astype(BF16)


def media_project(media, gains, attend, inner):
    rows, width = media.shape
    out = jax.ShapeDtypeStruct((rows, inner), BF16)
    block = pl.BlockSpec((PATCH_IMG, inner), lambda i: (i, 0))
    return pl.pallas_call(
        media_kernel,
        grid=(rows // PATCH_IMG,),
        out_shape=(out, out),
        in_specs=[
            pl.BlockSpec((PATCH_IMG, width), lambda i: (i, 0)),
            pl.BlockSpec(gains.shape, lambda i: (0, 0)),
            pl.BlockSpec((width, inner), lambda i: (0, 1)),
            pl.BlockSpec((width, inner), lambda i: (0, 2)),
        ],
        out_specs=(block, block),
        compiler_params=params(),
        cost_estimate=pl.CostEstimate(
            flops=4 * rows * width * inner, bytes_accessed=4 * rows * width, transcendentals=0
        ),
        name="media_project",
    )(media, gains, attend, attend)


def latent_kernel(l_ref, gb_ref, w_ref, q_ref, k_ref, v_ref):
    inner = q_ref.shape[1]
    hat, _ = normalise(l_ref[...])
    normed = (hat * gb_ref[1:2, :] + gb_ref[4:5, :]).astype(BF16)
    q_ref[...] = mm(normed, w_ref[:, :inner]).astype(BF16)
    k_ref[...] = mm(normed, w_ref[:, inner : 2 * inner]).astype(BF16)
    v_ref[...] = mm(normed, w_ref[:, 2 * inner : 3 * inner]).astype(BF16)


def latent_project(latents, gains, attend, inner):
    out = jax.ShapeDtypeStruct((latents.shape[0], inner), BF16)
    return pl.pallas_call(
        latent_kernel,
        out_shape=(out, out, out),
        in_specs=[vmem_spec()] * 3,
        out_specs=(vmem_spec(),) * 3,
        compiler_params=params(),
        name="latent_project",
    )(latents, gains, attend)


def head_mask(kind):
    rows = lax.broadcasted_iota(jnp.int32, (GROUP * HDIM, GROUP * HDIM), 0) // HDIM
    cols = lax.broadcasted_iota(jnp.int32, (GROUP * HDIM, GROUP * HDIM), 1) // HDIM
    return (rows == cols).astype(F32).astype(kind)


def spread_heads(queries, group, mask):
    width = GROUP * HDIM
    part = queries[:, group * width : (group + 1) * width]
    return jnp.concatenate([part] * GROUP, axis=0) * mask


def take_heads(full, mask):
    total = None
    for h in range(GROUP):
        part = slice(h * HDIM, (h + 1) * HDIM)
        term = full[part, :] * mask[part, :]
        total = term if total is None else total + term
    return total


def pack_columns(columns, first=0):
    rows = columns[0].shape[0]
    lane = lax.broadcasted_iota(jnp.int32, (rows, LANES), 1)
    tile = jnp.zeros((rows, LANES), F32)
    for h, column in enumerate(columns):
        tile = jnp.where(lane == first + h, column, tile)
    return tile


def expand_columns(tile, width):
    rows = tile.shape[0]
    head = lax.broadcasted_iota(jnp.int32, (rows, width), 1) // HDIM
    out = jnp.zeros((rows, width), F32)
    for h in range(width // HDIM):
        out = jnp.where(head == h, tile[:, h : h + 1], out)
    return out


def forward_kernel(
    ids, q0, q1, q2, q3, k_ref, v_ref, kl_ref, vl_ref, keep, send, keep_st, send_st, acc, tops, sums
):
    step = pl.program_id(0)
    clips = acc.shape[0]
    inner = acc.shape[2]
    groups = inner // (GROUP * HDIM)
    width = GROUP * HDIM
    mask = head_mask(F32)
    mask_half = mask.astype(BF16)

    def clip_queries(clip):
        parts = [q[clip] for q in (q0, q1, q2, q3)]
        return jnp.concatenate(parts, axis=0) * BF16(SCALE)

    def attend(clip, keys, values, fresh):
        queries = clip_queries(clip)
        new_tops, new_sums = [], []
        for g in range(groups):
            cols = slice(g * width, (g + 1) * width)
            scores = mm_nt(spread_heads(queries, g, mask_half), keys[:, cols])
            top = jnp.max(scores, axis=-1, keepdims=True)
            if not fresh:
                old_tile = tops[clip]
                old_top = jnp.concatenate(
                    [old_tile[:, g * GROUP + h : g * GROUP + h + 1] for h in range(GROUP)], axis=0
                )
                top = jnp.maximum(top, old_top)
            probs = jnp.exp(scores - top)
            total = jnp.sum(probs, axis=-1, keepdims=True)
            part = take_heads(mm(probs.astype(BF16), values[:, cols]), mask)
            if not fresh:
                old_tile = sums[clip]
                old_sum = jnp.concatenate(
                    [old_tile[:, g * GROUP + h : g * GROUP + h + 1] for h in range(GROUP)], axis=0
                )
                shrink = jnp.exp(old_top - top)
                total = total + old_sum * shrink
                part = part + acc[clip, :, cols] * take_heads(shrink, mask)
            acc[clip, :, cols] = part
            for h in range(GROUP):
                new_tops.append(top[h * HDIM : (h + 1) * HDIM])
                new_sums.append(total[h * HDIM : (h + 1) * HDIM])
        tops[clip] = pack_columns(new_tops)
        sums[clip] = pack_columns(new_sums)

    @pl.when(step == 0)
    def _():
        @pl.loop(0, clips)
        def _(clip):
            attend(clip, kl_ref[clip], vl_ref[clip], True)

    attend(ids[step], k_ref[...], v_ref[...], False)

    @pl.when(step == pl.num_programs(0) - 1)
    def _():
        rows = keep.shape[2]
        lane = lax.broadcasted_iota(jnp.int32, (HDIM, LANES), 1)

        @pl.loop(0, clips)
        def _(clip):
            total = jnp.where(lane < HEADS, sums[clip], 1.0)
            stat = tops[clip] + jnp.log(total)
            out = (acc[clip] / expand_columns(total, inner)).astype(BF16)
            for r in range(4):
                part = slice(r * rows, (r + 1) * rows)
                where_o, where_s = (send, send_st) if r % 2 else (keep, keep_st)
                where_o[r // 2, clip] = out[part]
                where_s[r // 2, clip] = stat[part]


def attention_forward(ids, queries, keys, values, latent_keys, latent_values):
    clips, rows, inner = queries[0].shape
    frames = keys.shape[0] // PATCH_IMG
    out = jax.ShapeDtypeStruct((2, clips, rows, inner), BF16)
    stat = jax.ShapeDtypeStruct((2, clips, rows, LANES), F32)
    block = pl.BlockSpec((PATCH_IMG, inner), lambda i, ids: (i, 0))

    def whole(shape):
        return pl.BlockSpec(shape, lambda i, ids: (0,) * len(shape))

    return pl.pallas_call(
        forward_kernel,
        grid_spec=pltpu.PrefetchScalarGridSpec(
            num_scalar_prefetch=1,
            grid=(frames,),
            in_specs=[whole((clips, rows, inner))] * 4
            + [block, block]
            + [whole((clips, rows, inner))] * 2,
            out_specs=(whole(out.shape), whole(out.shape), whole(stat.shape), whole(stat.shape)),
            scratch_shapes=[
                pltpu.VMEM((clips, 4 * rows, inner), F32),
                pltpu.VMEM((clips, 4 * rows, LANES), F32),
                pltpu.VMEM((clips, 4 * rows, LANES), F32),
            ],
        ),
        out_shape=(out, out, stat, stat),
        compiler_params=params(),
        name="attention_forward",
    )(ids, *queries, keys, values, latent_keys, latent_values)


def join_partials(first, first_stat, second, second_stat):
    width = first.shape[-1]
    top = jnp.maximum(first_stat, second_stat)
    total = jnp.exp(first_stat - top) + jnp.exp(second_stat - top)
    stat = top + jnp.log(total)
    out = first.astype(F32) * expand_columns(jnp.exp(first_stat - stat), width)
    out = out + second.astype(F32) * expand_columns(jnp.exp(second_stat - stat), width)
    return out, stat


def join_kernel(keep, keep_st, got, got_st, own, own_st, away, away_st):
    out, stat = join_partials(keep[0], keep_st[0], got[0], got_st[0])
    own[...] = out
    own_st[...] = stat
    out, stat = join_partials(keep[1], keep_st[1], got[1], got_st[1])
    away[...] = out.astype(BF16)
    away_st[...] = stat


def join_cores(keep, keep_st, got, got_st):
    _, rows, inner = keep.shape
    stat = jax.ShapeDtypeStruct((rows, LANES), F32)
    return pl.pallas_call(
        join_kernel,
        out_shape=(
            jax.ShapeDtypeStruct((rows, inner), F32),
            stat,
            jax.ShapeDtypeStruct((rows, inner), BF16),
            stat,
        ),
        in_specs=[vmem_spec()] * 4,
        out_specs=(vmem_spec(),) * 4,
        compiler_params=params(),
        name="join_cores",
    )(keep, keep_st, got, got_st)


class Gather:
    def __init__(self, depth, x_ref, o_ref, local_sem, send_sem, recv_sem, flips=()):
        self.depth = depth
        self.refs = x_ref, o_ref
        self.sems = local_sem, send_sem, recv_sem
        self.at = place()
        c = self.at[3]
        self.homes = [neighbours(*self.at, 1 if k in flips else c) for k in range(depth)]
        self.order = z_order(depth)

    def row(self, k, j):
        a, _, _, c = self.at
        _, b, e, _ = self.homes[k][j % 4]
        return flat((a - k) % self.depth, b, e, c if j < 4 else 1 - c)

    def copy(self, k, j):
        x_ref, o_ref = self.refs
        a, b, e, c = self.at
        base = {1: 0, 2: 0, 3: 1}.get(j, j - 4)
        if j == 0:
            target, row, src = ((a + k) % self.depth, b, e, c), flat(a, b, e, c), x_ref
        else:
            target = self.homes[k][min(j, 2)] if j < 4 else (a, b, e, 1 - c)
            row = self.row(k, base)
            src = x_ref if (k, base) == (0, 0) else o_ref.at[row]
        slot = k * 8 + j
        return pltpu.make_async_remote_copy(
            src_ref=src,
            dst_ref=o_ref.at[row],
            send_sem=self.sems[1].at[slot],
            recv_sem=self.sems[2].at[slot],
            device_id=device(*target),
            device_id_type=MESH,
        )

    def arrive(self, k, j):
        x_ref, o_ref = self.refs
        a, b, e, c = self.at
        slot = k * 8 + j
        pltpu.make_async_remote_copy(
            src_ref=x_ref,
            dst_ref=o_ref.at[self.row(k, j)],
            send_sem=self.sems[1].at[slot],
            recv_sem=self.sems[2].at[slot],
            device_id=device(a, b, e, 1 - c),
            device_id_type=MESH,
        ).wait_recv()

    def own(self):
        x_ref, o_ref = self.refs
        return pltpu.make_async_copy(x_ref, o_ref.at[flat(*self.at)], self.sems[0])

    def far(self, k):
        self.copy(k, 0).start()

    def begin(self):
        self.far(self.order[1])
        self.first(0)

    def settle(self, k=None):
        for k in self.order if k is None else [k]:
            for j in range(4, 8):
                self.arrive(k, j)
            if k == 0:
                self.own().wait()

    def first(self, k):
        if k:
            self.arrive(k, 0)
        for j in (1, 2, 4):
            self.copy(k, j).start()

    def second(self, k):
        self.arrive(k, 1)
        self.copy(k, 3).start()
        self.copy(k, 5).start()
        self.arrive(k, 2)
        self.copy(k, 6).start()

    def third(self, k):
        self.arrive(k, 3)
        self.copy(k, 7).start()

    def run(self, names):
        acts = {"z": self.far, "a": self.first, "b": self.second, "c": self.third}
        for name in names:
            acts[name[0]](self.order[int(name[1:])])

    def finish(self):
        for k in range(self.depth):
            for j in range(8):
                if k or j:
                    self.copy(k, j).wait_send()


def start_kernel(
    depth,
    w_ref,
    g_ref,
    b_ref,
    expand_ref,
    shrink_ref,
    output_ref,
    all_ref,
    shard_e,
    shard_s,
    gains_ref,
    shard,
    small,
    local_sem,
    send_sem,
    recv_sem,
    small_sem,
):
    rows, cols = w_ref.shape
    gather = Gather(depth, shard, all_ref, local_sem, send_sem, recv_sem)
    shard[:, :cols] = w_ref[...].astype(BF16)
    zeros = jnp.zeros((LANES - 6, rows), F32)
    lines = jnp.concatenate([g_ref[...], b_ref[...], zeros], axis=0)
    shard[:, cols:] = lines.T.astype(BF16)
    greet(depth, *gather.at)
    gather.own().start()
    gather.begin()
    gather.run(("z2", "z3"))
    width = output_ref.shape[1]
    groups = expand_ref.shape[1] // width
    for n in range(groups):
        shard_e[n * rows : (n + 1) * rows, :] = expand_ref[:, n * width : (n + 1) * width].astype(BF16)
    shard_e[groups * rows :, :] = output_ref[...].astype(BF16)
    shard_s[...] = shrink_ref[...].astype(BF16)
    gather.run(START_PLAN)
    gather.settle()
    load = pltpu.make_async_copy(all_ref.at[:, :, pl.ds(cols, LANES)], small, small_sem)
    load.start()
    load.wait()
    lines = small[...].reshape(depth * 8 * rows, LANES).astype(F32).T
    gains_ref[...] = lines[:8]
    gather.finish()


def start(weight, gains, biases, expand, shrink, output, depth):
    rows, cols = weight.shape
    count = depth * 8
    width = output.shape[1]
    rows_e = expand.shape[1] // width * rows + output.shape[0]
    return pl.pallas_call(
        functools.partial(start_kernel, depth),
        out_shape=(
            jax.ShapeDtypeStruct((count, rows, cols + LANES), BF16),
            jax.ShapeDtypeStruct((rows_e, width), BF16),
            jax.ShapeDtypeStruct(shrink.shape, BF16),
            jax.ShapeDtypeStruct((8, count * rows), F32),
        ),
        in_specs=[vmem_spec()] * 6,
        out_specs=(any_spec(), vmem_spec(), vmem_spec(), vmem_spec()),
        scratch_shapes=[
            pltpu.VMEM((rows, cols + LANES), BF16),
            pltpu.VMEM((count, rows, LANES), BF16),
            pltpu.SemaphoreType.DMA,
            pltpu.SemaphoreType.DMA((count,)),
            pltpu.SemaphoreType.DMA((count,)),
            pltpu.SemaphoreType.DMA,
        ],
        compiler_params=params(collective_id=1, has_side_effects=True),
        name="start",
    )(weight, gains, biases, expand, shrink, output)


def latent_mask(rows, inner):
    row = lax.broadcasted_iota(jnp.int32, (HEADS * rows, inner), 0) // rows
    col = lax.broadcasted_iota(jnp.int32, (HEADS * rows, inner), 1) // HDIM
    return (row == col).astype(F32)


def latent_attention(queries, keys, values, mask):
    rows = keys.shape[0]
    count = queries.shape[0]
    half = mask.astype(BF16)
    wide_k = jnp.concatenate([keys] * HEADS, axis=0) * half
    wide_v = jnp.concatenate([values] * HEADS, axis=0) * half
    scores = mm_nt(wide_k, queries).reshape(HEADS, rows, count)
    top = jnp.max(scores, axis=1, keepdims=True)
    probs = jnp.exp(scores - top)
    total = jnp.sum(probs, axis=1)
    out = mm_tn(probs.reshape(HEADS * rows, count).astype(BF16), wide_v)
    zeros = jnp.zeros((LANES - HEADS, count), F32)

    def tile(x):
        return jnp.concatenate([x, zeros], axis=0).T

    return out, tile(top.reshape(HEADS, count)), tile(total)


def remote_copy(src, dst, sems, slot, target):
    return pltpu.make_async_remote_copy(
        src_ref=src,
        dst_ref=dst,
        send_sem=sems[0].at[slot],
        recv_sem=sems[1].at[slot],
        device_id=device(*target),
        device_id_type=MESH,
    )


def feed_kernel(
    own,
    own_st,
    got,
    got_st,
    lat_ref,
    cot_ref,
    gb_ref,
    w_ref,
    out_ref,
    mixed_grad,
    context_grad,
    tile_ref,
    gain_ref,
    gw_ref,
    expand_v,
    shrink_v,
    output_v,
    grad_e,
    grad_s,
    grad_o,
    normed_v,
    normed_t,
    hat_v,
    acc_g,
    load_sem,
    store_sem,
):
    groups = expand_v.shape[0]
    width = expand_v.shape[3]
    blocks = expand_v.shape[1]
    shrink_rows = shrink_v.shape[1]
    per_group = blocks // groups
    expand_rows = expand_v.shape[2]
    shrink_at = groups * expand_rows
    output_at = shrink_at + shrink_rows
    output_rows = output_v.shape[1]
    half = width // 2
    inner = own.shape[1]

    def load_expand(g):
        return pltpu.make_async_copy(
            w_ref.at[:, pl.ds(g * expand_rows, expand_rows), :], expand_v.at[g], load_sem.at[g]
        )

    def load_shrink(g):
        part = pl.ds(g * per_group, per_group)
        return pltpu.make_async_copy(
            w_ref.at[part, pl.ds(shrink_at, shrink_rows), :],
            shrink_v.at[part],
            load_sem.at[groups + g],
        )

    load_output = pltpu.make_async_copy(
        w_ref.at[:, pl.ds(output_at, output_rows), :], output_v, load_sem.at[2 * groups]
    )
    load_output.start()
    for g in range(groups):
        load_expand(g).start()
        load_shrink(g).start()

    context, stat = join_partials(own[...], own_st[...], got[...], got_st[...])
    context_half = context.astype(BF16)
    load_output.wait()
    weight_o = output_v[...].reshape(inner, width)
    mixed = lat_ref[...] + mm(context_half, weight_o)
    hat, scale = normalise(mixed)
    hat_v[...] = hat
    normed = (hat * gb_ref[2:3, :] + gb_ref[5:6, :]).astype(BF16)
    normed_v[...] = normed
    normed_t[...] = normed.astype(F32).T.astype(BF16)
    out_ref[...] = mixed
    acc_g[...] = jnp.zeros_like(acc_g)

    def store_e(s, slot):
        return pltpu.make_async_copy(
            grad_e.at[slot],
            gw_ref.at[:, pl.ds((s // 2) * expand_rows, expand_rows), pl.ds((s % 2) * half, half)],
            store_sem.at[slot],
        )

    def store_s(s, slot):
        rows = half // shrink_rows
        return pltpu.make_async_copy(
            grad_s.at[slot],
            gw_ref.at[pl.ds(s * rows, rows), pl.ds(shrink_at, shrink_rows), :],
            store_sem.at[2 + slot],
        )

    cot = cot_ref[...]
    steps = 2 * groups
    for s in range(steps):
        g, slot = s // 2, s % 2
        if slot == 0:
            load_expand(g).wait()
            load_shrink(g).wait()
        cols = slice(slot * half, (slot + 1) * half)
        w_e = expand_v[g, :, :, cols].reshape(blocks * expand_rows, half)
        first = s * half // shrink_rows
        w_s = shrink_v[first : first + half // shrink_rows].reshape(half, width)
        pre = mm(normed_v[...], w_e)
        cdf = 0.5 * (1.0 + lax.erf(pre * (0.5**0.5)))
        hidden = (pre * cdf).astype(BF16)
        out_ref[...] += mm(hidden, w_s)
        grad_hidden = mm_nt(cot, w_s)
        pdf = jnp.exp(-0.5 * pre * pre) * (1.0 / math.sqrt(2.0 * math.pi))
        grad_pre = (grad_hidden * (cdf + pre * pdf)).astype(BF16)
        if s >= 2:
            store_e(s - 2, slot).wait()
            store_s(s - 2, slot).wait()
        grad_s[slot] = mm_tn(hidden, cot).astype(BF16).reshape(half // shrink_rows, shrink_rows, width)
        grad_e[slot] = (
            mm(normed_t[...], grad_pre).astype(BF16).reshape(blocks, expand_rows, half)
        )
        store_e(s, slot).start()
        store_s(s, slot).start()
        acc_g[...] += mm_nt(grad_pre, w_e)

    grad_normed = acc_g[...]
    hat = hat_v[...]
    rows = gain_ref.shape[0]
    gain_ref[...] = jnp.concatenate(
        [
            jnp.sum(grad_normed * hat, axis=0, keepdims=True),
            jnp.sum(grad_normed, axis=0, keepdims=True),
            jnp.zeros((rows - 2, width), F32),
        ],
        axis=0,
    )
    total = cot.astype(F32) + norm_back(grad_normed, hat, scale, gb_ref[2:3, :])
    mixed_grad[...] = total
    attended = total.astype(BF16)
    grad_o[...] = mm_tn(context_half, attended).astype(BF16).reshape(grad_o.shape)
    store_o = pltpu.make_async_copy(
        grad_o, gw_ref.at[:, pl.ds(output_at, output_rows), :], store_sem.at[4]
    )
    store_o.start()
    grad_c = mm_nt(attended, weight_o).astype(BF16)
    context_grad[...] = grad_c
    product = grad_c.astype(F32) * context
    head = lax.broadcasted_iota(jnp.int32, product.shape, 1) // HDIM
    deltas = [
        jnp.sum(jnp.where(head == h, product, 0.0), axis=-1, keepdims=True) for h in range(HEADS)
    ]
    lane = lax.broadcasted_iota(jnp.int32, stat.shape, 1)
    tile_ref[...] = jnp.where(lane < HEADS, stat, pack_columns(deltas, HEADS))
    for s in range(steps - 2, steps):
        store_e(s, s % 2).wait()
        store_s(s, s % 2).wait()
    store_o.wait()


def feed_forward(own, own_st, got, got_st, latents, cotangent, gains, weights):
    rows, width = latents.shape
    inner = own.shape[1]
    blocks = weights.shape[0]
    ff = 4 * width
    groups = ff // width
    expand_rows = width // blocks
    shrink_rows = ff // blocks
    output_rows = inner // blocks
    half = width // 2
    flops = 2 * rows * (6 * width * ff + 3 * width * inner)
    return pl.pallas_call(
        feed_kernel,
        out_shape=(
            jax.ShapeDtypeStruct((rows, width), F32),
            jax.ShapeDtypeStruct((rows, width), F32),
            jax.ShapeDtypeStruct((rows, inner), BF16),
            jax.ShapeDtypeStruct((rows, LANES), F32),
            jax.ShapeDtypeStruct((8, width), F32),
            jax.ShapeDtypeStruct(weights.shape, BF16),
        ),
        in_specs=[vmem_spec()] * 7 + [any_spec()],
        out_specs=(vmem_spec(),) * 5 + (any_spec(),),
        scratch_shapes=[
            pltpu.VMEM((groups, blocks, expand_rows, width), BF16),
            pltpu.VMEM((blocks, shrink_rows, width), BF16),
            pltpu.VMEM((blocks, output_rows, width), BF16),
            pltpu.VMEM((2, blocks, expand_rows, half), BF16),
            pltpu.VMEM((2, half // shrink_rows, shrink_rows, width), BF16),
            pltpu.VMEM((blocks, output_rows, width), BF16),
            pltpu.VMEM((rows, width), BF16),
            pltpu.VMEM((width, rows), BF16),
            pltpu.VMEM((rows, width), F32),
            pltpu.VMEM((rows, width), F32),
            pltpu.SemaphoreType.DMA((2 * groups + 1,)),
            pltpu.SemaphoreType.DMA((5,)),
        ],
        compiler_params=params(),
        cost_estimate=pl.CostEstimate(
            flops=flops, bytes_accessed=4 * weights.size, transcendentals=2 * rows * ff
        ),
        name="feed_forward",
    )(own, own_st, got, got_st, latents, cotangent, gains, weights)


def backward_kernel(
    ids,
    q0,
    q1,
    q2,
    q3,
    g0,
    g1,
    g2,
    g3,
    t0,
    t1,
    t2,
    t3,
    k_ref,
    v_ref,
    kl_ref,
    vl_ref,
    m_ref,
    gb_ref,
    wk_ref,
    wv_ref,
    media_grad,
    latent_kv,
    keep,
    send,
    weight_grad,
    gain_ref,
    acc,
):
    step = pl.program_id(0)
    clips = acc.shape[0]
    inner = acc.shape[2]
    groups = inner // (GROUP * HDIM)
    width = GROUP * HDIM
    mask = head_mask(F32)
    mask_half = mask.astype(BF16)

    def attend(clip, keys, values, fresh):
        queries = jnp.concatenate([q[clip] for q in (q0, q1, q2, q3)], axis=0) * BF16(SCALE)
        grads = jnp.concatenate([g[clip] for g in (g0, g1, g2, g3)], axis=0)
        stats = jnp.concatenate([t[clip] for t in (t0, t1, t2, t3)], axis=0).T
        key_parts, value_parts = [], []
        for g in range(groups):
            cols = slice(g * width, (g + 1) * width)

            def line(first):
                at = first + g * GROUP
                return jnp.concatenate([stats[at + h : at + h + 1, :] for h in range(GROUP)], axis=1)

            wide_q = spread_heads(queries, g, mask_half)
            wide_g = spread_heads(grads, g, mask_half)
            probs = jnp.exp(mm_nt(keys[:, cols], wide_q) - line(0))
            grad_probs = mm_nt(values[:, cols], wide_g)
            grad_scores = (probs * (grad_probs - line(HEADS))).astype(BF16)
            key_parts.append(mm(grad_scores, wide_q))
            value_parts.append(mm(probs.astype(BF16), wide_g))
            part = take_heads(mm_tn(grad_scores, keys[:, cols]), mask)
            if fresh:
                acc[clip, :, cols] = part
            else:
                acc[clip, :, cols] += part
        return jnp.concatenate(key_parts + value_parts, axis=1).astype(BF16)

    @pl.when(step == 0)
    def _():
        gain_ref[...] = jnp.zeros_like(gain_ref)
        weight_grad[...] = jnp.zeros_like(weight_grad)

        @pl.loop(0, clips)
        def _(clip):
            latent_kv[clip] = attend(clip, kl_ref[clip], vl_ref[clip], True)

    grad_kv = attend(ids[step], k_ref[...], v_ref[...], False)
    hat, scale = normalise(m_ref[...].astype(F32))
    gain = gb_ref[0:1, :]
    normed = (hat * gain + gb_ref[3:4, :]).astype(BF16)
    weight_grad[...] += mm_tn(normed, grad_kv)
    grad = mm_nt(grad_kv[:, :inner], wk_ref[...]) + mm_nt(grad_kv[:, inner:], wv_ref[...])
    gain_ref[0:1, :] += jnp.sum(grad * hat, axis=0, keepdims=True)
    gain_ref[1:2, :] += jnp.sum(grad, axis=0, keepdims=True)
    media_grad[...] = norm_back(grad, hat, scale, gain).astype(BF16)

    @pl.when(step == pl.num_programs(0) - 1)
    def _():
        rows = keep.shape[2]

        @pl.loop(0, clips)
        def _(clip):
            out = (acc[clip] * SCALE).astype(BF16)
            for r in range(4):
                part = slice(r * rows, (r + 1) * rows)
                where_o = send if r % 2 else keep
                where_o[r // 2, clip] = out[part]


def attention_backward(
    ids, queries, grads, tiles, keys, values, latent_keys, latent_values, media, gains, attend
):
    clips, rows, inner = queries[0].shape
    width = media.shape[1]
    frames = keys.shape[0] // PATCH_IMG
    block = pl.BlockSpec((PATCH_IMG, inner), lambda i, ids: (i, 0))
    wide = pl.BlockSpec((PATCH_IMG, width), lambda i, ids: (i, 0))

    def whole(shape):
        return pl.BlockSpec(shape, lambda i, ids: (0,) * len(shape))

    def column(n):
        return pl.BlockSpec((width, inner), lambda i, ids: (0, n))

    query = whole((clips, rows, inner))
    pair = (2, clips, rows, inner)
    return pl.pallas_call(
        backward_kernel,
        grid_spec=pltpu.PrefetchScalarGridSpec(
            num_scalar_prefetch=1,
            grid=(frames,),
            in_specs=[query] * 8
            + [whole((clips, rows, LANES))] * 4
            + [block, block, query, query, wide, whole(gains.shape), column(1), column(2)],
            out_specs=(
                wide,
                whole((clips, rows, 2 * inner)),
                whole(pair),
                whole(pair),
                whole((width, 2 * inner)),
                whole((8, width)),
            ),
            scratch_shapes=[pltpu.VMEM((clips, 4 * rows, inner), F32)],
        ),
        out_shape=(
            jax.ShapeDtypeStruct(media.shape, BF16),
            jax.ShapeDtypeStruct((clips, rows, 2 * inner), BF16),
            jax.ShapeDtypeStruct(pair, BF16),
            jax.ShapeDtypeStruct(pair, BF16),
            jax.ShapeDtypeStruct((width, 2 * inner), F32),
            jax.ShapeDtypeStruct((8, width), F32),
        ),
        compiler_params=params(),
        name="attention_backward",
    )(
        ids,
        *queries,
        *grads,
        *tiles,
        keys,
        values,
        latent_keys,
        latent_values,
        media,
        gains,
        attend,
        attend,
    )


def last_kernel(
    lat_ref, mixed_grad, first, second, kv_ref, gb_ref, w_ref, gw_ref, gm_ref, gf_ref, out_ref, pack_ref
):
    inner = first.shape[1]
    width = lat_ref.shape[1]
    hat, scale = normalise(lat_ref[...])
    gain = gb_ref[1:2, :]
    normed = (hat * gain + gb_ref[4:5, :]).astype(BF16)
    grad_q = (first[...].astype(F32) + second[...].astype(F32)).astype(BF16)
    grad_kv = kv_ref[...]
    grad = mm_nt(grad_q, w_ref[:, :inner]) + mm_nt(grad_kv, w_ref[:, inner : 3 * inner])
    pack_ref[:, :inner] = mm_tn(normed, grad_q).astype(BF16)
    pack_ref[:, inner : 3 * inner] = (gw_ref[...] + mm_tn(normed, grad_kv)).astype(BF16)
    lines = jnp.concatenate(
        [
            gm_ref[0:1, :],
            jnp.sum(grad * hat, axis=0, keepdims=True),
            gf_ref[0:1, :],
            gm_ref[1:2, :],
            jnp.sum(grad, axis=0, keepdims=True),
            gf_ref[1:2, :],
            jnp.zeros((LANES - 6, width), F32),
        ],
        axis=0,
    )
    pack_ref[:, 3 * inner :] = lines.T.astype(BF16)
    out_ref[...] = mixed_grad[...] + norm_back(grad, hat, scale, gain)


def latent_backward(latents, mixed_grad, first, second, grad_kv, gains, attend, grad_w, gain_m, gain_f):
    return pl.pallas_call(
        last_kernel,
        out_shape=(
            jax.ShapeDtypeStruct(latents.shape, F32),
            jax.ShapeDtypeStruct(attend.shape, BF16),
        ),
        in_specs=[vmem_spec()] * 10,
        out_specs=(vmem_spec(), vmem_spec()),
        compiler_params=params(),
        name="latent_backward",
    )(latents, mixed_grad, first, second, grad_kv, gains, attend, grad_w, gain_m, gain_f)


class Scatter:
    def __init__(self, depth, chunk, g_ref, buffers, load_sem, sems, flips=()):
        self.depth = depth
        self.chunk = chunk
        self.g_ref = g_ref
        self.own, self.from_c, self.from_two, self.from_one, self.from_z = buffers
        self.load_sem = load_sem
        self.sems = sems
        self.at = place()
        a, b, e, c = self.at
        self.flips = flips
        self.homes = [neighbours(*self.at, 1 if k in flips else c) for k in range(depth)]
        self.twin = (a, b, e, 1 - c)
        self.order = z_order(depth)[::-1]

    def row(self, k, j, core):
        _, b, e, _ = self.homes[k][j]
        return flat((self.at[0] + k) % self.depth, b, e, core)

    def load(self, k, j):
        slot = k * 4 + j
        src = self.g_ref.at[self.row(k, j, self.at[3])]
        return pltpu.make_async_copy(src, self.own.at[slot], self.load_sem.at[slot])

    def to_twin(self, k, j):
        there = j if k in self.flips else (0, 2, 1, 3)[j]
        src = self.g_ref.at[self.row(k, there, 1 - self.at[3])]
        return remote_copy(src, self.from_c.at[k * 4 + j], self.sems, k * 8 + j, self.twin)

    def to_two(self, k, j):
        spot = self.from_two.at[k * 2 + j - 2]
        return remote_copy(self.own.at[k * 4 + j], spot, self.sems, k * 8 + 2 + j, self.homes[k][2])

    def to_one(self, k):
        return remote_copy(
            self.own.at[k * 4 + 1], self.from_one.at[k], self.sems, k * 8 + 6, self.homes[k][1]
        )

    def to_far(self, k):
        a, b, e, c = self.at
        target = ((a + k) % self.depth, b, e, c)
        return remote_copy(
            self.own.at[k * 4], self.from_z.at[k - 1], self.sems, k * 8 + 7, target
        )

    def add(self, slot, spot):
        mine = self.own.at[slot]
        add_into(mine, mine, spot, self.chunk)

    def begin(self):
        for k in self.order:
            for j in (3, 2, 1, 0):
                self.load(k, j).start()
                self.to_twin(k, j).start()

    def first(self, k):
        for j in (3, 2, 1, 0):
            self.load(k, j).wait()
            self.to_twin(k, j).wait_recv()
            self.add(k * 4 + j, self.from_c.at[k * 4 + j])
            if j >= 2:
                self.to_two(k, j).start()

    def second(self, k):
        for j in (3, 2):
            self.to_two(k, j).wait_recv()
            self.add(k * 4 + j - 2, self.from_two.at[k * 2 + j - 2])
            if j == 3:
                self.to_one(k).start()

    def third(self, k):
        self.to_one(k).wait_recv()
        self.add(k * 4, self.from_one.at[k])
        if k:
            self.to_far(k).start()

    def run(self, names):
        acts = {"a": self.first, "b": self.second, "c": self.third}
        for name in names:
            acts[name[0]](self.order[int(name[1:])])

    def finish(self, o_ref):
        for k in range(1, self.depth):
            self.to_far(k).wait_recv()

        @pl.loop(0, o_ref.shape[1] // self.chunk)
        def _(step):
            part = pl.ds(pl.multiple_of(step * self.chunk, self.chunk), self.chunk)
            total = self.own[0, :, part].astype(F32)
            for k in range(1, self.depth):
                total = total + self.from_z[k - 1, :, part].astype(F32)
            o_ref[:, part] = total

        for k in range(self.depth):
            for j in range(4):
                self.to_twin(k, j).wait_send()
            self.to_two(k, 3).wait_send()
            self.to_two(k, 2).wait_send()
            self.to_one(k).wait_send()
            if k:
                self.to_far(k).wait_send()


def scatter_buffers(depth, rows, cols):
    def slots(n):
        return pltpu.VMEM((n, rows, cols), BF16)

    return [slots(depth * 4), slots(depth * 4), slots(depth * 2), slots(depth), slots(depth - 1)]


def scatter_sems(depth):
    return [
        pltpu.SemaphoreType.DMA((depth * 4,)),
        pltpu.SemaphoreType.DMA((depth * 8,)),
        pltpu.SemaphoreType.DMA((depth * 8,)),
    ]


def latent_attention_back(queries, grads, stats, keys, values, mask):
    rows = keys.shape[0]
    count = queries.shape[0]
    half = mask.astype(BF16)
    wide_k = jnp.concatenate([keys] * HEADS, axis=0) * half
    wide_v = jnp.concatenate([values] * HEADS, axis=0) * half
    cut = (HEADS, rows, count)
    scores = mm_nt(wide_k, queries).reshape(cut)
    probs = jnp.exp(scores - stats[:HEADS][:, None, :])
    grad_probs = mm_nt(wide_v, grads).reshape(cut)
    grad_scores = probs * (grad_probs - stats[HEADS : 2 * HEADS][:, None, :])
    grad_scores = grad_scores.reshape(HEADS * rows, count).astype(BF16)
    probs = probs.reshape(HEADS * rows, count).astype(BF16)

    def fold(full):
        full = full * mask
        total = full[:rows]
        for h in range(1, HEADS):
            total = total + full[h * rows : (h + 1) * rows]
        return total

    grad_kv = [fold(mm(grad_scores, queries)), fold(mm(probs, grads))]
    return mm_tn(grad_scores, wide_k), jnp.concatenate(grad_kv, axis=1).astype(BF16)


def to_lines(tile):
    return tile.T[: 2 * HEADS]


def from_lines(lines):
    zeros = jnp.zeros((LANES - lines.shape[0], lines.shape[1]), F32)
    return jnp.concatenate([lines, zeros], axis=0).T


def back_kernel(
    depth,
    frames,
    chunk,
    plan,
    ids,
    last,
    has,
    same,
    g_ref,
    q_ref,
    context_grad,
    tile_ref,
    k_ref,
    v_ref,
    m_ref,
    kl_ref,
    vl_ref,
    gb_ref,
    w_ref,
    lat_ref,
    mixed_ref,
    gain_f,
    media_grad,
    latents_grad,
    pack_ref,
    mine_ref,
    own,
    from_c,
    from_two,
    from_one,
    from_z,
    load_sem,
    send_sem,
    recv_sem,
    all_g,
    lines,
    tiles,
    weight_acc,
    gain_acc,
    outs,
    latent_kv,
    keep,
    send,
    core_q,
    away,
    y_q,
    link_send,
    link_recv,
    mixed_sem,
):
    step = pl.program_id(0)
    a, b, e, c = place()
    twin, other = (a, b, e, 1 - c), (a, b, 1 - e, c)
    links = link_send, link_recv
    buffers = own, from_c, from_two, from_one, from_z
    scatter = Scatter(depth, chunk, g_ref, buffers, load_sem, (send_sem, recv_sem), BACK_FLIPS)
    clips, rows, inner = kl_ref.shape
    total_rows = clips * rows
    groups = inner // (GROUP * HDIM)
    width = GROUP * HDIM
    mask = head_mask(F32)
    mask_half = mask.astype(BF16)
    grad_copies = [
        remote_copy(all_g.at[0], all_g.at[2], links, 0, other),
        remote_copy(all_g.at[0], all_g.at[1], links, 1, twin),
        remote_copy(all_g.at[2], all_g.at[3], links, 2, twin),
    ]
    line_copies = [
        remote_copy(lines.at[0], lines.at[2], links, 3, other),
        remote_copy(lines.at[0], lines.at[1], links, 4, twin),
        remote_copy(lines.at[2], lines.at[3], links, 5, twin),
    ]
    core_copy = remote_copy(send, core_q, links, 6, twin)
    y_copy = remote_copy(away, y_q, links, 7, other)

    def clip_queries(clip):
        return jnp.concatenate([q_ref[r, clip] for r in range(4)], axis=0) * BF16(SCALE)

    def clip_grads(clip):
        return jnp.concatenate([all_g[r, clip] for r in range(4)], axis=0)

    def clip_stats(clip):
        return jnp.concatenate([tiles[r, clip] for r in range(4)], axis=0).T

    @pl.when(step == 0)
    def _():
        all_g[0] = context_grad[...]
        lines[0] = to_lines(tile_ref[...])
        greet(depth, a, b, e, c)
        for copies in (grad_copies, line_copies):
            copies[0].start()
            copies[1].start()
        scatter.begin()
        gain_acc[...] = jnp.zeros_like(gain_acc)
        weight_acc[...] = jnp.zeros_like(weight_acc)
        outs[0] = jnp.zeros_like(outs[0])

    for when, names in plan[:-2]:

        @pl.when(step == when)
        def _(names=names):
            scatter.run(names)

    @pl.when(step == 0)
    def _():
        for copies in (grad_copies, line_copies):
            copies[0].wait()
            copies[2].start()
        for copies in (grad_copies, line_copies):
            copies[1].wait()
            copies[2].wait()
        for r in range(4):
            tiles[r] = from_lines(lines[r]).reshape(clips, rows, LANES)

    @pl.when((step >= 1) & (step <= frames))
    def _():
        frame = step - 1
        before = jnp.maximum(frame - 1, 0)
        clip = ids[frame]
        joined = same[frame] == 1
        queries, grads, stats = clip_queries(clip), clip_grads(clip), clip_stats(clip)
        key_parts, value_parts = [], []
        for g in range(groups):
            cols = slice(g * width, (g + 1) * width)

            def line(first):
                at = first + g * GROUP
                return jnp.concatenate([stats[at + h : at + h + 1, :] for h in range(GROUP)], axis=1)

            wide_q = spread_heads(queries, g, mask_half)
            wide_g = spread_heads(grads, g, mask_half)
            keys = k_ref[:, cols]
            probs = jnp.exp(mm_nt(keys, wide_q) - line(0))
            grad_probs = mm_nt(v_ref[:, cols], wide_g)
            grad_scores = (probs * (grad_probs - line(HEADS))).astype(BF16)
            key_parts.append(mm(grad_scores, wide_q))
            value_parts.append(mm(probs.astype(BF16), wide_g))
            part = take_heads(mm_tn(grad_scores, keys), mask)
            outs[frame, :, cols] = part + jnp.where(joined, outs[before, :, cols], 0.0)
        grad_kv = jnp.concatenate(key_parts + value_parts, axis=1).astype(BF16)
        hat, scale = normalise(m_ref[...].astype(F32))
        gain = gb_ref[0:1, :]
        normed = (hat * gain + gb_ref[3:4, :]).astype(BF16)
        weight_acc[...] += mm_tn(normed, grad_kv)
        grad = mm_nt(grad_kv, w_ref[:, inner : 3 * inner])
        gain_acc[0:1, :] += jnp.sum(grad * hat, axis=0, keepdims=True)
        gain_acc[1:2, :] += jnp.sum(grad, axis=0, keepdims=True)
        media_grad[...] = norm_back(grad, hat, scale, gain).astype(BF16)

    @pl.when(step == frames + 1)
    def _():
        wide = latent_mask(rows, inner)

        def one_clip(clip):
            out, grad_kv = latent_attention_back(
                clip_queries(clip),
                clip_grads(clip),
                clip_stats(clip),
                kl_ref[clip],
                vl_ref[clip],
                wide,
            )
            out = (out + jnp.where(has[clip] == 1, outs[last[clip]], 0.0)) * SCALE
            return out, grad_kv

        @pl.loop(0, clips // TOGETHER)
        def _(index):
            some = [index * TOGETHER + n for n in range(TOGETHER)]
            results = [one_clip(clip) for clip in some]
            for clip, (out, grad_kv) in zip(some, results):
                latent_kv[clip] = grad_kv
                for r in range(4):
                    part = slice(r * rows, (r + 1) * rows)
                    if r % 2:
                        send[r // 2, clip] = out[part].astype(BF16)
                    else:
                        keep[r // 2, clip] = out[part]

        core_copy.start()
        hat, scale = normalise(lat_ref[...])
        gain = gb_ref[1:2, :]
        normed = (hat * gain + gb_ref[4:5, :]).astype(BF16)
        core_copy.wait()
        away[...] = (keep[1] + core_q[1].astype(F32)).astype(BF16)
        y_copy.start()
        grad_kv = latent_kv[...].reshape(total_rows, 2 * inner)
        pack_ref[:, inner : 3 * inner] = (weight_acc[...] + mm_tn(normed, grad_kv)).astype(BF16)
        grad = mm_nt(grad_kv, w_ref[:, inner : 3 * inner])
        mixed = weight_acc.at[:total_rows]
        load_mixed = pltpu.make_async_copy(mixed_ref, mixed, mixed_sem)
        load_mixed.start()
        scatter.run(plan[-2][1])
        y_copy.wait()
        grad_q = (keep[0] + core_q[0].astype(F32) + y_q[...].astype(F32)).astype(BF16)
        grad_q = grad_q.reshape(total_rows, inner)
        grad = grad + mm_nt(grad_q, w_ref[:, :inner])
        pack_ref[:, :inner] = mm_tn(normed, grad_q).astype(BF16)
        table = jnp.concatenate(
            [
                gain_acc[0:1, :],
                jnp.sum(grad * hat, axis=0, keepdims=True),
                gain_f[0:1, :],
                gain_acc[1:2, :],
                jnp.sum(grad, axis=0, keepdims=True),
                gain_f[1:2, :],
                jnp.zeros((LANES - 6, grad.shape[1]), F32),
            ],
            axis=0,
        )
        pack_ref[:, 3 * inner :] = table.T.astype(BF16)
        load_mixed.wait()
        latents_grad[...] = mixed[...] + norm_back(grad, hat, scale, gain)
        scatter.run(plan[-1][1])
        scatter.finish(mine_ref)


def back(
    ids,
    last,
    has,
    same,
    grad_feed,
    query_all,
    context_grad,
    tile,
    keys,
    values,
    media,
    latent_key,
    latent_value,
    gains,
    attend,
    latents,
    mixed_grad,
    gain_f,
    depth,
    chunk,
    plan,
):
    clips, rows, inner = latent_key.shape
    frames = media.shape[0] // PATCH_IMG
    width = media.shape[1]
    total = clips * rows
    cut = (clips, rows, inner)
    _, feed_rows, feed_cols = grad_feed.shape
    once = pl.Buffered(buffer_count=1)

    def whole(x):
        return pl.BlockSpec(x.shape, lambda i: (0,) * len(x.shape), pipeline_mode=once)

    def block(columns):
        return pl.BlockSpec((PATCH_IMG, columns), lambda i: (jnp.clip(i - 1, 0, frames - 1), 0))

    smem = pl.BlockSpec(memory_space=pltpu.SMEM)
    outs = (
        jax.ShapeDtypeStruct(media.shape, BF16),
        jax.ShapeDtypeStruct(latents.shape, F32),
        jax.ShapeDtypeStruct(attend.shape, BF16),
        jax.ShapeDtypeStruct((feed_rows, feed_cols), F32),
    )
    return pl.pallas_call(
        functools.partial(back_kernel, depth, frames, chunk, plan),
        grid=(frames + 2,),
        out_shape=outs,
        in_specs=[smem] * 4
        + [any_spec(), whole(query_all), whole(context_grad), whole(tile)]
        + [block(inner), block(inner), block(width)]
        + [whole(x) for x in (latent_key, latent_value, gains, attend, latents)]
        + [any_spec(), whole(gain_f)],
        out_specs=(block(width),) + tuple(whole(x) for x in outs[1:]),
        scratch_shapes=scatter_buffers(depth, feed_rows, feed_cols)
        + scatter_sems(depth)
        + [
            pltpu.VMEM((4,) + cut, BF16),
            pltpu.VMEM((4, 2 * HEADS, total), F32),
            pltpu.VMEM((4, clips, rows, LANES), F32),
            pltpu.VMEM((width, 2 * inner), F32),
            pltpu.VMEM((8, width), F32),
            pltpu.VMEM((frames, 4 * rows, inner), F32),
            pltpu.VMEM((clips, rows, 2 * inner), BF16),
            pltpu.VMEM((2,) + cut, F32),
            pltpu.VMEM((2,) + cut, BF16),
            pltpu.VMEM((2,) + cut, BF16),
            pltpu.VMEM(cut, BF16),
            pltpu.VMEM(cut, BF16),
            pltpu.SemaphoreType.DMA((8,)),
            pltpu.SemaphoreType.DMA((8,)),
            pltpu.SemaphoreType.DMA,
        ],
        compiler_params=params(collective_id=4, has_side_effects=True),
        name="back",
    )(
        ids,
        last,
        has,
        same,
        grad_feed,
        query_all,
        context_grad,
        tile,
        keys,
        values,
        media,
        latent_key,
        latent_value,
        gains,
        attend,
        latents,
        mixed_grad,
        gain_f,
    )


def head_kernel(
    depth,
    frames,
    parts,
    plan,
    late,
    ids,
    last,
    has,
    same,
    shard_e,
    shard_s,
    m_ref,
    lat_ref,
    cot_ref,
    gb_ref,
    wq_ref,
    k_ref,
    v_ref,
    q_ref,
    kl_ref,
    vl_ref,
    out_ref,
    mixed_grad,
    context_grad,
    tile_ref,
    gain_ref,
    gw_ref,
    all_k,
    all_v,
    all_q,
    outs,
    tops,
    sums,
    keep,
    keep_st,
    send,
    send_st,
    core_o,
    send_li,
    core_li,
    away,
    y_o,
    away_li,
    y_li,
    weights_e,
    weights_s,
    grad_s,
    grad_o,
    normed_v,
    normed_t,
    hat_v,
    local_sem,
    send_e,
    recv_e,
    send_s,
    recv_s,
    link_send,
    link_recv,
    out_sem,
    store_sem,
):
    step = pl.program_id(0)
    a, b, e, c = place()
    twin, other = (a, b, e, 1 - c), (a, b, 1 - e, c)
    links = link_send, link_recv
    gather_e = Gather(depth, shard_e, weights_e, local_sem.at[0], send_e, recv_e, HEAD_FLIPS)
    gather_s = Gather(depth, shard_s, weights_s, local_sem.at[1], send_s, recv_s, HEAD_FLIPS)
    clips, rows, inner = kl_ref.shape
    total_rows = clips * rows
    groups = inner // (GROUP * HDIM)
    width = GROUP * HDIM
    slabs = PATCH_IMG // all_k.shape[1]
    mask = head_mask(F32)
    mask_half = mask.astype(BF16)
    query_copies = [
        remote_copy(all_q.at[0], all_q.at[2], links, 0, other),
        remote_copy(all_q.at[0], all_q.at[1], links, 1, twin),
        remote_copy(all_q.at[2], all_q.at[3], links, 2, twin),
    ]
    share = clips // parts
    lot = share * rows

    def core_copies(p):
        some = pl.ds(p * share, share)
        return [
            remote_copy(send.at[:, some], core_o.at[:, some], links, 3 + 4 * p, twin),
            remote_copy(send_li.at[p], core_li.at[p], links, 4 + 4 * p, twin),
        ]

    def y_copies(p):
        some = pl.ds(p * lot, lot)
        return [
            remote_copy(away.at[some], y_o.at[some], links, 5 + 4 * p, other),
            remote_copy(away_li.at[p], y_li.at[p], links, 6 + 4 * p, other),
        ]

    def join_part(p):
        some = slice(p * share, (p + 1) * share)
        for copy in core_copies(p):
            copy.wait()
        for n in (1, 0):
            out, stat = join_partials(
                keep[n, some].reshape(lot, inner),
                keep_st[n, some].reshape(lot, LANES),
                core_o[n, some].reshape(lot, inner),
                from_lines(core_li[p, n]),
            )
            if n:
                away[p * lot : (p + 1) * lot] = out.astype(BF16)
                away_li[p] = to_lines(stat)
                for copy in y_copies(p):
                    copy.start()
            else:
                keep[0, some] = out.reshape(share, rows, inner)
                keep_st[0, some] = stat.reshape(share, rows, LANES)

    keep_queries = pltpu.make_async_copy(all_q, q_ref, out_sem)

    def run(names):
        for name in names:
            (gather_e if name[0] == "e" else gather_s).run((name[1:],))

    def clip_queries(clip):
        return jnp.concatenate([all_q[r, clip] for r in range(4)], axis=0) * BF16(SCALE)

    @pl.when(step == 0)
    def _():
        greet(depth, a, b, e, c)
        hat, _ = normalise(lat_ref[...])
        normed = (hat * gb_ref[1:2, :] + gb_ref[4:5, :]).astype(BF16)
        all_q[0] = mm(normed, wq_ref[:, :inner]).astype(BF16).reshape(clips, rows, inner)
        query_copies[0].start()
        query_copies[1].start()
        gather_s.own().start()
        gather_e.own().start()
        gather_e.begin()
        kl_ref[...] = (
            mm(normed, wq_ref[:, inner : 2 * inner]).astype(BF16).reshape(clips, rows, inner)
        )
        vl_ref[...] = (
            mm(normed, wq_ref[:, 2 * inner : 3 * inner]).astype(BF16).reshape(clips, rows, inner)
        )
        outs[0] = jnp.zeros_like(outs[0])
        tops[0] = jnp.zeros_like(tops[0])
        sums[0] = jnp.zeros_like(sums[0])

    @pl.when(step < frames)
    def _():
        hat, _ = normalise(m_ref[...].astype(F32))
        normed = (hat * gb_ref[0:1, :] + gb_ref[3:4, :]).astype(BF16)
        new_k = mm(normed, wq_ref[:, inner : 2 * inner]).astype(BF16)
        new_v = mm(normed, wq_ref[:, 2 * inner : 3 * inner]).astype(BF16)
        k_ref[...] = new_k
        v_ref[...] = new_v
        at = pl.ds(step * slabs, slabs)
        all_k[at] = new_k.reshape(slabs, PATCH_IMG // slabs, inner)
        all_v[at] = new_v.reshape(slabs, PATCH_IMG // slabs, inner)

    for when, names in plan:

        @pl.when(step == when)
        def _(names=names):
            run(names)

    @pl.when(step == frames // 2)
    def _():
        query_copies[0].wait()
        query_copies[2].start()

    @pl.when(step == frames)
    def _():
        query_copies[1].wait()
        query_copies[2].wait()
        keep_queries.start()

    @pl.when((step >= frames) & (step < 2 * frames))
    def _():
        frame = step - frames
        before = jnp.maximum(frame - 1, 0)
        queries = clip_queries(ids[frame])
        joined = same[frame] == 1
        old_tops = jnp.where(joined, tops[before], MASKED)
        old_sums = jnp.where(joined, sums[before], 0.0)
        at = pl.ds(frame * slabs, slabs)
        new_tops, new_sums = [], []
        for g in range(groups):
            cols = slice(g * width, (g + 1) * width)

            def column(tile):
                first = g * GROUP
                return jnp.concatenate(
                    [tile[:, first + h : first + h + 1] for h in range(GROUP)], axis=0
                )

            keys = all_k[at, :, cols].reshape(PATCH_IMG, width)
            values = all_v[at, :, cols].reshape(PATCH_IMG, width)
            scores = mm_nt(spread_heads(queries, g, mask_half), keys)
            old_top = column(old_tops)
            top = jnp.maximum(jnp.max(scores, axis=-1, keepdims=True), old_top)
            probs = jnp.exp(scores - top)
            shrink = jnp.exp(old_top - top)
            total = jnp.sum(probs, axis=-1, keepdims=True) + column(old_sums) * shrink
            part = take_heads(mm(probs.astype(BF16), values), mask)
            old = jnp.where(joined, outs[before, :, cols], 0.0)
            outs[frame, :, cols] = part + old * take_heads(shrink, mask)
            for h in range(GROUP):
                new_tops.append(top[h * HDIM : (h + 1) * HDIM])
                new_sums.append(total[h * HDIM : (h + 1) * HDIM])
        tops[frame] = pack_columns(new_tops)
        sums[frame] = pack_columns(new_sums)

    @pl.when((step >= 2 * frames) & (step < 2 * frames + parts))
    def _():
        wide = latent_mask(rows, inner)
        lane = lax.broadcasted_iota(jnp.int32, (4 * rows, LANES), 1)
        first = (step - 2 * frames) * share

        def one_clip(clip):
            out, top, total = latent_attention(clip_queries(clip), kl_ref[clip], vl_ref[clip], wide)
            at = last[clip]
            there = has[clip] == 1
            far_top = jnp.where(there, tops[at], MASKED)
            far_sum = jnp.where(there, sums[at], 0.0)
            far_out = jnp.where(there, outs[at], 0.0)
            both = jnp.maximum(top, far_top)
            near, far = jnp.exp(top - both), jnp.exp(far_top - both)
            total = jnp.where(lane < HEADS, total * near + far_sum * far, 1.0)
            stat = both + jnp.log(total)
            out = out * expand_columns(near / total, inner)
            return out + far_out * expand_columns(far / total, inner), stat

        @pl.loop(0, share // TOGETHER)
        def _(index):
            some = [first + index * TOGETHER + n for n in range(TOGETHER)]
            results = [one_clip(clip) for clip in some]
            for clip, (out, stat) in zip(some, results):
                for r in range(4):
                    part = slice(r * rows, (r + 1) * rows)
                    if r % 2:
                        send[r // 2, clip] = out[part].astype(BF16)
                        send_st[r // 2, clip] = stat[part]
                    else:
                        keep[r // 2, clip] = out[part]
                        keep_st[r // 2, clip] = stat[part]

    for p in range(parts):

        @pl.when(step == 2 * frames + p)
        def _(p=p):
            for n in range(2):
                some = slice(p * share, (p + 1) * share)
                send_li[p, n] = to_lines(send_st[n, some].reshape(lot, LANES))
            for copy in core_copies(p):
                copy.start()
            if p:
                join_part(p - 1)

    @pl.when(step == 2 * frames + parts)
    def _():
        run(late[0])
        join_part(parts - 1)
        run(late[1])
        gather_e.settle()
        run(late[2])
        for p in range(parts):
            for copy in y_copies(p):
                copy.wait()
        stat_y = jnp.concatenate([from_lines(y_li[p]) for p in range(parts)], axis=0)
        context, stat = join_partials(
            keep[0].reshape(total_rows, inner),
            keep_st[0].reshape(total_rows, LANES),
            y_o[...],
            stat_y,
        )
        feed_part(
            functools.partial(run_late, run, late[3:], gather_s),
            context,
            stat,
            depth,
            a,
            gather_s.order,
            lat_ref,
            cot_ref,
            gb_ref,
            weights_e,
            weights_s,
            out_ref,
            mixed_grad,
            context_grad,
            tile_ref,
            gain_ref,
            gw_ref,
            all_k,
            grad_s,
            grad_o,
            normed_v,
            normed_t,
            hat_v,
            store_sem,
        )
        keep_queries.wait()
        gather_e.finish()
        gather_s.finish()


def run_late(run, late, gather, n):
    run(late[n])
    gather.settle(gather.order[n])


def feed_part(
    ready,
    context,
    stat,
    depth,
    plane,
    order,
    lat_ref,
    cot_ref,
    gb_ref,
    weights_e,
    weights_s,
    out_ref,
    mixed_grad,
    context_grad,
    tile_ref,
    gain_ref,
    gw_ref,
    grad_e,
    grad_s,
    grad_o,
    normed_v,
    normed_t,
    hat_v,
    store_sem,
):
    blocks, shrink_rows, width = weights_s.shape
    per_plane = blocks // depth
    inner = context.shape[1]
    output_rows = inner // blocks
    expand_rows = (weights_e.shape[1] - output_rows) // depth
    shrink_at = depth * expand_rows
    output_at = shrink_at + shrink_rows
    half = width // 2
    half_rows = half // shrink_rows
    context_half = context.astype(BF16)

    def weight_o():
        return weights_e[:, shrink_at : shrink_at + output_rows, :].reshape(inner, width)

    mixed = lat_ref[...] + mm(context_half, weight_o())
    hat, scale = normalise(mixed)
    hat_v[...] = hat
    normed = (hat * gb_ref[2:3, :] + gb_ref[5:6, :]).astype(BF16)
    normed_v[...] = normed
    normed_t[...] = normed.astype(F32).T.astype(BF16)
    out_ref[...] = mixed
    mixed_grad[...] = jnp.zeros_like(mixed_grad)
    cot = cot_ref[...]
    stores = []
    for n, k in enumerate(order):
        ready(n)
        plane_k = (plane - k) % depth
        e_rows = pl.ds(pl.multiple_of(plane_k * expand_rows, expand_rows), expand_rows)
        for slot in range(2):
            cols = slice(slot * half, (slot + 1) * half)
            w_e = weights_e[:, e_rows, cols].reshape(blocks * expand_rows, half)
            s_rows = pl.ds(plane_k * per_plane + slot * half_rows, half_rows)
            w_s = weights_s[s_rows].reshape(half, width)
            pre = mm(normed_v[...], w_e)
            cdf = 0.5 * (1.0 + lax.erf(pre * (0.5**0.5)))
            hidden = (pre * cdf).astype(BF16)
            out_ref[...] += mm(hidden, w_s)
            grad_hidden = mm_nt(cot, w_s)
            pdf = jnp.exp(-0.5 * pre * pre) * (1.0 / math.sqrt(2.0 * math.pi))
            grad_pre = (grad_hidden * (cdf + pre * pdf)).astype(BF16)
            if n:
                for copy in stores[2 * (2 * n + slot) - 4 : 2 * (2 * n + slot) - 2]:
                    copy.wait()
            grad_s[slot] = mm_tn(hidden, cot).astype(BF16).reshape(half_rows, shrink_rows, width)
            e_spot = grad_e.at[pl.ds(slot * blocks, blocks)]
            e_spot[...] = (
                mm(normed_t[...], grad_pre).astype(BF16).reshape(blocks, expand_rows, half)
            )
            stores += [
                pltpu.make_async_copy(
                    e_spot, gw_ref.at[:, e_rows, pl.ds(slot * half, half)], store_sem.at[slot]
                ),
                pltpu.make_async_copy(
                    grad_s.at[slot],
                    gw_ref.at[s_rows, pl.ds(shrink_at, shrink_rows), :],
                    store_sem.at[2 + slot],
                ),
            ]
            stores[-1].start()
            stores[-2].start()
            mixed_grad[...] += mm_nt(grad_pre, w_e)

    grad_normed = mixed_grad[...]
    hat = hat_v[...]
    rows = gain_ref.shape[0]
    gain_ref[...] = jnp.concatenate(
        [
            jnp.sum(grad_normed * hat, axis=0, keepdims=True),
            jnp.sum(grad_normed, axis=0, keepdims=True),
            jnp.zeros((rows - 2, width), F32),
        ],
        axis=0,
    )
    total = cot.astype(F32) + norm_back(grad_normed, hat, scale, gb_ref[2:3, :])
    mixed_grad[...] = total
    attended = total.astype(BF16)
    grad_o[...] = mm_tn(context_half, attended).astype(BF16).reshape(grad_o.shape)
    store_o = pltpu.make_async_copy(
        grad_o, gw_ref.at[:, pl.ds(output_at, output_rows), :], store_sem.at[4]
    )
    store_o.start()
    grad_c = mm_nt(attended, weight_o()).astype(BF16)
    context_grad[...] = grad_c
    product = grad_c.astype(F32) * context
    head = lax.broadcasted_iota(jnp.int32, product.shape, 1) // HDIM
    deltas = [
        jnp.sum(jnp.where(head == h, product, 0.0), axis=-1, keepdims=True) for h in range(HEADS)
    ]
    lane = lax.broadcasted_iota(jnp.int32, stat.shape, 1)
    tile_ref[...] = jnp.where(lane < HEADS, stat, pack_columns(deltas, HEADS))
    for copy in stores[-4:]:
        copy.wait()
    store_o.wait()


def head(
    ids,
    last,
    has,
    same,
    shard_e,
    shard_s,
    media,
    latents,
    cotangent,
    gains,
    attend,
    clips,
    inner,
    depth,
    parts,
    plan,
    late,
):
    rows = latents.shape[0] // clips
    frames = media.shape[0] // PATCH_IMG
    width = media.shape[1]
    total = clips * rows
    cut = (clips, rows, inner)
    count = depth * 8
    expand_rows = (shard_e.shape[0] - inner // count) // depth
    feed_rows = shard_e.shape[0] + shard_s.shape[0]
    slabs = PATCH_IMG // expand_rows * frames
    half_rows = width // 2 // shard_s.shape[0]
    once = pl.Buffered(buffer_count=1)

    def whole(x):
        return pl.BlockSpec(x.shape, lambda i: (0,) * len(x.shape), pipeline_mode=once)

    def block(columns):
        return pl.BlockSpec((PATCH_IMG, columns), lambda i: (jnp.minimum(i, frames - 1), 0))

    smem = pl.BlockSpec(memory_space=pltpu.SMEM)
    kv = jax.ShapeDtypeStruct((media.shape[0], inner), BF16)
    small = jax.ShapeDtypeStruct(cut, BF16)
    outs = (
        small,
        small,
        jax.ShapeDtypeStruct((total, width), F32),
        jax.ShapeDtypeStruct((total, width), F32),
        jax.ShapeDtypeStruct((total, inner), BF16),
        jax.ShapeDtypeStruct((total, LANES), F32),
        jax.ShapeDtypeStruct((8, width), F32),
    )
    lines = (2 * HEADS, total // parts)
    dma = pltpu.SemaphoreType.DMA
    return pl.pallas_call(
        functools.partial(head_kernel, depth, frames, parts, plan, late),
        grid=(2 * frames + parts + 1,),
        out_shape=(kv, kv, jax.ShapeDtypeStruct((4,) + cut, BF16))
        + outs
        + (jax.ShapeDtypeStruct((count, feed_rows, width), BF16),),
        in_specs=[smem] * 4
        + [any_spec(), any_spec(), block(width)]
        + [whole(x) for x in (latents, cotangent, gains, attend)],
        out_specs=(block(inner), block(inner), any_spec())
        + tuple(whole(x) for x in outs)
        + (any_spec(),),
        scratch_shapes=[
            pltpu.VMEM((slabs, expand_rows, inner), BF16),
            pltpu.VMEM((slabs, expand_rows, inner), BF16),
            pltpu.VMEM((4,) + cut, BF16),
            pltpu.VMEM((frames, 4 * rows, inner), F32),
            pltpu.VMEM((frames, 4 * rows, LANES), F32),
            pltpu.VMEM((frames, 4 * rows, LANES), F32),
            pltpu.VMEM((2,) + cut, F32),
            pltpu.VMEM((2, clips, rows, LANES), F32),
            pltpu.VMEM((2,) + cut, BF16),
            pltpu.VMEM((2, clips, rows, LANES), F32),
            pltpu.VMEM((2,) + cut, BF16),
            pltpu.VMEM((parts, 2) + lines, F32),
            pltpu.VMEM((parts, 2) + lines, F32),
            pltpu.VMEM((total, inner), BF16),
            pltpu.VMEM((total, inner), BF16),
            pltpu.VMEM((parts,) + lines, F32),
            pltpu.VMEM((parts,) + lines, F32),
            pltpu.VMEM((count,) + shard_e.shape, BF16),
            pltpu.VMEM((count,) + shard_s.shape, BF16),
            pltpu.VMEM((2, half_rows) + shard_s.shape, BF16),
            pltpu.VMEM((count, inner // count, width), BF16),
            pltpu.VMEM((total, width), BF16),
            pltpu.VMEM((width, total), BF16),
            pltpu.VMEM((total, width), F32),
            dma((2,)),
            dma((count,)),
            dma((count,)),
            dma((count,)),
            dma((count,)),
            dma((3 + 4 * parts,)),
            dma((3 + 4 * parts,)),
            dma,
            dma((5,)),
        ],
        compiler_params=params(collective_id=2, has_side_effects=True),
        name="head",
    )(ids, last, has, same, shard_e, shard_s, media, latents, cotangent, gains, attend)


def norm_kernel(depth, images, lats, chunk, pack_ref, feed_ref, norm_ref, mine_ref, *refs):
    buffers, refs = refs[:5], refs[5:]
    load_sem, send_sem, recv_sem, tile, slots, tile_send, tile_recv = refs
    count = images * lats
    img = lax.axis_index("img")
    lat = lax.axis_index("lat")
    me = img * lats + lat
    scatter = Scatter(depth, chunk, pack_ref, buffers, load_sem, (send_sem, recv_sem))
    barrier = pltpu.get_barrier_semaphore()

    def other(k):
        there = (me + k) % count
        return there // lats, there % lats

    for k in range(1, count):
        pl.semaphore_signal(barrier, inc=1, device_id=other(k), device_id_type=MESH)
    pl.semaphore_wait(barrier, count - 1)
    scatter.begin()
    feed_rows = feed_ref.shape[0]
    squares = jnp.zeros((8, feed_ref.shape[1]), F32)
    for n in range(feed_rows // 8):
        part = feed_ref[n * 8 : (n + 1) * 8, :]
        squares = squares + part * part
    squares = jnp.sum(squares)
    scatter.run(NORM_PLAN)
    scatter.finish(mine_ref)
    own = mine_ref[...]
    tile[...] = jnp.full(tile.shape, squares + jnp.sum(own * own), F32)
    slots[me] = tile[...]

    def exchange(k, spot):
        return pltpu.make_async_remote_copy(
            src_ref=tile,
            dst_ref=slots.at[spot],
            send_sem=tile_send.at[k],
            recv_sem=tile_recv.at[k],
            device_id=other(k),
            device_id_type=MESH,
        )

    for k in range(1, count):
        exchange(k, me).start()
    for k in range(1, count):
        exchange(k, (me - k) % count).wait_recv()
    norm_ref[...] = jnp.sqrt(jnp.sum(slots[...], axis=0))
    for k in range(1, count):
        exchange(k, me).wait_send()


def norm_and_sum(grad_attend, mine_feed, images, lats):
    count = images * lats
    depth = images // 2
    rows = grad_attend.shape[0] // count
    cols = grad_attend.shape[1]
    tile = (8, LANES)
    return pl.pallas_call(
        functools.partial(norm_kernel, depth, images, lats, cols),
        out_shape=(jax.ShapeDtypeStruct(tile, F32), jax.ShapeDtypeStruct((rows, cols), F32)),
        in_specs=[any_spec(), vmem_spec()],
        out_specs=(vmem_spec(), vmem_spec()),
        scratch_shapes=scatter_buffers(depth, rows, cols)
        + scatter_sems(depth)
        + [
            pltpu.VMEM(tile, F32),
            pltpu.VMEM((count,) + tile, F32),
            pltpu.SemaphoreType.DMA((count,)),
            pltpu.SemaphoreType.DMA((count,)),
        ],
        compiler_params=params(collective_id=3, has_side_effects=True),
        name="norm",
    )(grad_attend.reshape(count, rows, cols), mine_feed)


def update_kernel(rates, inner, count, norm_ref, mine, feed_ref, *refs):
    states, refs = refs[:18], refs[18:]
    olds, refs = refs[:count], refs[count:]
    norm_out, news, moved = refs[0], refs[1:19], refs[19:]
    for old, new in zip(olds, moved):
        new[...] = old[...]

    @pl.when(pl.program_id(0) == 0)
    def _():
        update_states(rates, inner, norm_ref, mine, feed_ref, states, norm_out, news)


def update_states(rates, inner, norm_ref, mine, feed_ref, states, norm_out, news):
    norm = norm_ref[...]
    norm_out[...] = norm
    factor = jnp.minimum(1.0, CLIP_NORM / (norm + 1e-06))[0:1, 0:1]

    def update(n, grad, rows, cols, decay):
        at = (rows, cols)
        master = states[n][at]
        step_grad = factor * grad
        if decay:
            step_grad = step_grad + decay * master
        buffer = MOMENTUM * states[6 + n][at] + step_grad
        new = master - rates[n] * (step_grad + MOMENTUM * buffer)
        news[n][at] = new
        news[6 + n][at] = buffer
        news[12 + n][at] = AVERAGING * states[12 + n][at] + (1.0 - AVERAGING) * new

    every = slice(None)
    width = feed_ref.shape[1]
    expand_rows, expand_cols = states[2].shape
    shrink_rows = states[3].shape[0]
    at = expand_cols // width * expand_rows
    update(0, mine[:, : 3 * inner], every, every, DECAY)
    update(1, feed_ref[at + shrink_rows :, :], every, every, DECAY)
    for g in range(expand_cols // width):
        grad = feed_ref[g * expand_rows : (g + 1) * expand_rows, :]
        update(2, grad, every, slice(g * width, (g + 1) * width), DECAY)
    update(3, feed_ref[at : at + shrink_rows, :], every, every, DECAY)
    small = mine[:, 3 * inner :].T
    update(4, small[0:3], every, every, 0.0)
    update(5, small[3:6], every, every, 0.0)


def update_all(norm, mine, mine_feed, states, rates, inner, moved, steps):
    def like(x):
        return jax.ShapeDtypeStruct(x.shape, x.dtype)

    def whole(x):
        return pl.BlockSpec(x.shape, lambda i: (0, 0), pipeline_mode=pl.Buffered(buffer_count=1))

    def block(x):
        return pl.BlockSpec((x.shape[0] // steps, x.shape[1]), lambda i: (i, 0))

    blocks = [block(x) for x in moved]
    kept = [whole(x) for x in states]
    return pl.pallas_call(
        functools.partial(update_kernel, rates, inner, len(moved)),
        grid=(steps,),
        out_shape=(like(norm),) + tuple(like(x) for x in states) + tuple(like(x) for x in moved),
        in_specs=[whole(norm), whole(mine), whole(mine_feed)] + kept + blocks,
        out_specs=tuple([whole(norm)] + kept + blocks),
        compiler_params=params(),
        name="update",
    )(norm, mine, mine_feed, *states, *moved)


def pack_feed(expand, shrink, output):
    width = shrink.shape[-1]
    groups = expand.shape[-1] // width
    lead = expand.shape[:-2]
    rows = expand.shape[-2]
    cut = expand.reshape(lead + (rows, groups, width))
    cut = jnp.moveaxis(cut, -2, -3).reshape(lead + (groups * rows, width))
    return jnp.concatenate([cut, shrink, output], axis=-2)


def unpack_feed(packed, rows, shrink_rows):
    width = packed.shape[-1]
    lead = packed.shape[:-2]
    groups = (packed.shape[-2] - shrink_rows) // rows
    split = groups * rows
    cut = packed[..., :split, :].reshape(lead + (groups, rows, width))
    expand = jnp.moveaxis(cut, -3, -2).reshape(lead + (rows, groups * width))
    return (
        expand,
        packed[..., split : split + shrink_rows, :],
        packed[..., split + shrink_rows :, :],
    )


def step_size(width, inner, ff):
    return 0.37 * math.sqrt((4 * width * inner + 2 * width * ff) / width)


def lat_pairs(count, along_core):
    pairs = []
    for lat in range(count):
        e, c = lat // 2, lat % 2
        pairs.append((lat, e * 2 + 1 - c if along_core else (1 - e) * 2 + c))
    return pairs


def shards(
    images,
    lats,
    media,
    latents,
    counts,
    cotangent,
    attend_weight,
    output_weight,
    expand_weight,
    shrink_weight,
    layer_gains,
    layer_biases,
    attend_momentum,
    output_momentum,
    expand_momentum,
    shrink_momentum,
    gains_momentum,
    biases_momentum,
    attend_average,
    output_average,
    expand_average,
    shrink_average,
    gains_average,
    biases_average,
):
    devices = images * lats
    depth = images // 2
    fast = devices == BLOCKS and lats == 4 and images % 2 == 0
    samples, lat_dev, width = latents.shape
    rows = samples * lat_dev
    ff = expand_weight.shape[1]
    inner = attend_weight.shape[1] // 3
    patch_dev = media.shape[0]
    frames = patch_dev // PATCH_IMG
    over_core = functools.partial(lax.ppermute, axis_name="lat", perm=lat_pairs(lats, True))
    over_y = functools.partial(lax.ppermute, axis_name="lat", perm=lat_pairs(lats, False))

    attend_rows = attend_weight.shape[0]
    if fast:
        attend, shard_e, shard_s, gains = start(
            attend_weight,
            layer_gains.T,
            layer_biases.T,
            expand_weight,
            shrink_weight,
            output_weight,
            depth,
        )
        attend = attend.reshape(width, attend.shape[2])
    else:

        def everywhere(x):
            return lax.all_gather(x.astype(BF16), AXES, axis=0, tiled=True)

        small = jnp.concatenate([layer_gains, layer_biases], axis=1)
        small = jnp.pad(small, ((0, 0), (0, LANES - small.shape[1])))
        attend = everywhere(jnp.concatenate([attend_weight, small], axis=1))
        feed = pack_feed(
            everywhere(expand_weight).reshape(BLOCKS, width // BLOCKS, ff),
            everywhere(shrink_weight).reshape(BLOCKS, ff // BLOCKS, width),
            everywhere(output_weight).reshape(BLOCKS, inner // BLOCKS, width),
        )
        gains = attend[:, 3 * inner : 3 * inner + 8].astype(F32).T

    sample_ends = jnp.cumsum(counts[0])
    first_frame = lax.axis_index("lat") * frames
    frame_ids = first_frame + jnp.arange(frames, dtype=jnp.int32)
    ids = jnp.sum((frame_ids[:, None] >= sample_ends[None, :]).astype(jnp.int32), axis=1)
    ids = jnp.clip(ids, 0, samples - 1)

    latent_flat = latents.reshape(rows, width)
    cot_flat = cotangent.reshape(rows, width)
    cut = (samples, lat_dev, inner)

    def to_group(own):
        other = over_y(own)
        return [own, over_core(own), other, over_core(other)]

    if fast:
        clip = jnp.arange(samples, dtype=jnp.int32)
        here = ids[None, :] == clip[:, None]
        has = jnp.any(here, axis=1).astype(jnp.int32)
        last = jnp.max(jnp.where(here, jnp.arange(frames, dtype=jnp.int32)[None, :], 0), axis=1)
        same = jnp.concatenate([jnp.zeros((1,), jnp.int32), (ids[1:] == ids[:-1]).astype(jnp.int32)])
        (
            keys,
            values,
            query_all,
            latent_key,
            latent_value,
            out_rows,
            mixed_grad,
            context_grad,
            tile,
            gain_f,
            grad_feed,
        ) = head(
            ids,
            last,
            has,
            same,
            shard_e,
            shard_s,
            media,
            latent_flat,
            cot_flat,
            gains,
            attend,
            samples,
            inner,
            depth,
            3,
            HEAD_PLAN,
            HEAD_LATE,
        )
    else:
        query, latent_key, latent_value = latent_project(latent_flat, gains, attend, inner)
        latent_key = latent_key.reshape(cut)
        latent_value = latent_value.reshape(cut)
        queries = to_group(query.reshape(cut))
        keys, values = media_project(media, gains, attend, inner)
        keep, send, keep_st, send_st = attention_forward(
            ids, queries, keys, values, latent_key, latent_value
        )
        got, got_st = over_core(send), over_core(send_st)
        flat_o, flat_s = (2, rows, inner), (2, rows, LANES)
        own, own_st, away, away_st = join_cores(
            keep.reshape(flat_o),
            keep_st.reshape(flat_s),
            got.reshape(flat_o),
            got_st.reshape(flat_s),
        )
        got, got_st = over_y(away), over_y(away_st)
        out_rows, mixed_grad, context_grad, tile, gain_f, grad_feed = feed_forward(
            own, own_st, got, got_st, latent_flat, cot_flat, gains, feed
        )
    if fast:
        grad_media, latents_grad, grad_attend, mine_feed = back(
            ids,
            last,
            has,
            same,
            grad_feed,
            query_all,
            context_grad.reshape(cut),
            tile,
            keys,
            values,
            media,
            latent_key,
            latent_value,
            gains,
            attend,
            latent_flat,
            mixed_grad,
            gain_f,
            depth,
            2 * LANES,
            BACK_PLAN,
        )
    else:
        grads = to_group(context_grad.reshape(cut))
        tiles = to_group(tile.reshape(samples, lat_dev, LANES))
        grad_media, latent_kv, keep, send, grad_kv, gain_m = attention_backward(
            ids,
            queries,
            grads,
            tiles,
            keys,
            values,
            latent_key,
            latent_value,
            media,
            gains,
            attend,
        )
        got = over_core(send)
        pair = keep.astype(F32) + got.astype(F32)
        got = over_y(pair[1].astype(BF16))
        latents_grad, grad_attend = latent_backward(
            latent_flat,
            mixed_grad,
            pair[0].reshape(rows, inner),
            got.reshape(rows, inner),
            latent_kv.reshape(rows, 2 * inner),
            gains,
            attend,
            grad_kv,
            gain_m,
            gain_f,
        )

        def owners(x):
            return lax.psum_scatter(x.astype(F32), AXES, scatter_dimension=0, tiled=True)

        mine = owners(grad_attend)
        own_expand, own_shrink, own_output = unpack_feed(grad_feed, width // BLOCKS, ff // BLOCKS)
        own_expand = owners(own_expand.reshape(width, ff))
        own_shrink = owners(own_shrink.reshape(ff, width))
        own_output = owners(own_output.reshape(inner, width))
    masters = (
        attend_weight,
        output_weight,
        expand_weight,
        shrink_weight,
        layer_gains,
        layer_biases,
    )
    moments = (
        attend_momentum,
        output_momentum,
        expand_momentum,
        shrink_momentum,
        gains_momentum,
        biases_momentum,
    )
    averages = (
        attend_average,
        output_average,
        expand_average,
        shrink_average,
        gains_average,
        biases_average,
    )
    step_rate = step_size(width, inner, ff)
    if fast:
        rates = tuple(step_rate * scale for scale in RATE_SCALES)
        states = masters + moments + averages
        states = tuple(x.T if x.shape[1] == 3 else x for x in states)
        norm, mine = norm_and_sum(grad_attend, mine_feed, images, lats)
        norm, *news = update_all(
            norm,
            mine,
            mine_feed,
            states,
            rates,
            inner,
            (),
            1,
        )
        news = [x.T if x.shape[0] == 3 else x for x in news[:18]]
        grad_norm = norm[0, 0]
        new_masters, new_buffers, new_smoothed = news[:6], news[6:12], news[12:]
    else:
        small = mine[:, 3 * inner :]
        owned = (
            mine[:, : 3 * inner],
            own_output,
            own_expand,
            own_shrink,
            small[:, 0:3],
            small[:, 3:6],
        )
        squares = sum(jnp.sum(piece * piece) for piece in owned)
        squares = lax.psum(squares, AXES)
        grad_norm = jnp.sqrt(squares)
        factor = jnp.minimum(1.0, CLIP_NORM / (grad_norm + 1e-06))
        decay_rates = (DECAY, DECAY, DECAY, DECAY, 0.0, 0.0)
        new_masters = []
        new_buffers = []
        new_smoothed = []
        for master, moment, average, reduced, decay_rate, rate_scale in zip(
            masters, moments, averages, owned, decay_rates, RATE_SCALES
        ):
            step_grad = factor * reduced + decay_rate * master
            buffer = MOMENTUM * moment + step_grad
            master_new = master - step_rate * rate_scale * (step_grad + MOMENTUM * buffer)
            new_masters.append(master_new)
            new_buffers.append(buffer)
            new_smoothed.append(AVERAGING * average + (1.0 - AVERAGING) * master_new)
    return (
        out_rows.reshape(latents.shape),
        grad_media,
        latents_grad.reshape(latents.shape),
        grad_norm,
        *new_masters,
        *new_buffers,
        *new_smoothed,
    )


def solution(mesh):
    rows = P(AXES, None)
    split = P("img", "lat", None)
    return jax.shard_map(
        functools.partial(shards, mesh.shape["img"], mesh.shape["lat"]),
        mesh=mesh,
        in_specs=(rows, split, P("img", None), split) + (rows,) * 18,
        out_specs=(split, rows, split, P()) + (rows,) * 18,
        check_vma=False,
    )
```

profile of v0, /device:TPU:0, one launch (start us, length us, event | category | flops | bytes accessed | tf_op | source)
XLA Modules:
  0.0 318.7 jit_solution(11494544431129822971)
XLA Ops:
  0.7 0.7 copy.46
  1.5 0.1 reduce
  1.6 0.2 convert_reduce_fusion
  1.8 0.0 copy-start.2
  1.8 0.6 select_reduce_fusion.last
  2.4 0.1 slice_compare_fusion
  2.4 0.6 add_convert_fusion.same
  3.0 0.1 fusion
  3.1 0.5 convert_element_type.8.has
  3.6 33.8 %start.1 = (bf16[32,32,1664]{2,1,0:T(8,128)(2,1)}, bf16[144,1024]{1,0:T(8,128)(2,1)}, bf16[128,1024]{1,0:T(8,128)(2,1)}, f32[8,1024]{1,0:T(8,128)}) custom-call(f32[32,1536]{1,0:T(8,128)} %refs_0_.1, f32[3,32]{1,0:T(4,128)} %bitcast.30, f32[3,32]{1,0:T(4,128)} %bitcast.32, f32[32,4096]{1,0:T(8,128)} %refs_2_.1, f32[128,1024]{1,0:T(8,128)} %refs_3_.1, ...), custom_call_target="tpu_custom_call" | custom-call | tf_op jit(solution)/shard_map/start/pallas_call | solution.py:505
  37.4 0.0 copy-done.2
  37.4 126.4 %head.1 = (bf16[3072,512]{1,0:T(8,128)(2,1)}, bf16[3072,512]{1,0:T(8,128)(2,1)}, bf16[4,24,16,512]{3,2,1,0:T(8,128)(2,1)}, bf16[24,16,512]{2,1,0:T(8,128)(2,1)},...) custom-call(s32[12]{0:T(128)} %copy-done.2, ...), custom_call_target="tpu_custom_call" | custom-call | tf_op jit(solution)/shard_map/head/pallas_call | solution.py:1910
  163.9 107.8 %back.1 = (bf16[3072,1024]{1,0:T(8,128)(2,1)}, f32[384,1024]{1,0:T(8,128)}, bf16[1024,1664]{1,0:T(8,128)(2,1)}, f32[272,1024]{1,0:T(8,128)}) custom-call(s32[12]{0:T(128)} %copy-done.2, s32[24]{0:T(128)} %select_reduce_fusion.last, s32[24]{0:T(128)} %convert_element_type.8.has, s32[12]{0:T(128)} %add_convert_fusion.same, ...), custom_call_target="tpu_custom_call" | custom-call | tf_op jit(solution)/shard_map/back/pallas_call | solution.py:1374
  271.7 31.9 %norm.1 = (f32[8,128]{1,0:T(8,128)}, f32[32,1664]{1,0:T(8,128)}) custom-call(bf16[32,32,1664]{2,1,0:T(8,128)(2,1)} %bitcast.25, f32[272,1024]{1,0:T(8,128)} %get-tuple-element.80.feed_ref), custom_call_target="tpu_custom_call" | custom-call | tf_op jit(solution)/shard_map/norm/pallas_call | solution.py:2017
  303.7 0.0 copy-start
  303.7 4.9 %update.1 = (f32[8,128]{1,0:T(8,128)}, f32[32,1536]{1,0:T(8,128)}, f32[16,1024]{1,0:T(8,128)}, f32[32,4096]{1,0:T(8,128)}, f32[128,1024]{1,0:T(8,128)}, /*index=...) custom-call(f32[8,128]{1,0:T(8,128)} %get-tuple-element.81.norm_ref,, ...), custom_call_target="tpu_custom_call" | custom-call | tf_op jit(solution)/shard_map/update/pallas_call | solution.py:2092
  308.6 1.2 slice.11
  309.8 0.0 copy-done
  309.8 1.1 copy.50
  311.0 0.0 copy-start.1
  311.0 6.3 %copy.51 = bf16[3072,1024]{1,0:T(8,128)(2,1)} copy(bf16[3072,1024]{1,0:T(8,128)(2,1)} %get-tuple-element.125) | data formatting | bytes 12582912
  317.3 0.0 copy-done.1
  317.3 1.1 copy.52
  (3 shorter events, 0.1 us)
Async XLA Ops:
  1.8 35.7 %copy-start.2 = (s32[12]{0:T(128)}, s32[12]{0:T(128)S(1)}, u32[]{:S(2)}) copy-start(s32[12]{0:T(128)S(1)} %broadcast_clamp_fusion.ids) | copy-start | bytes 148
  303.7 6.2 %copy-start = (f32[384,1024]{1,0:T(8,128)S(1)}, f32[384,1024]{1,0:T(8,128)}, u32[]{:S(2)}) copy-start(f32[384,1024]{1,0:T(8,128)} %get-tuple-element.66) | copy-start | bytes 4718596
  311.0 6.3 %copy-start.1 = (f32[384,1024]{1,0:T(8,128)S(1)}, f32[384,1024]{1,0:T(8,128)}, u32[]{:S(2)}) copy-start(f32[384,1024]{1,0:T(8,128)} %get-tuple-element.78) | copy-start | bytes 4718596
where the time goes:
time: 319 us
  Pallas kernels  305 us (96%)
  local copies, waits for them, and re-layouts  10.6 us (3%)
    pallas_call x1, Pallas kernels, head(): pl.pallas_call(functools.partial(head_kernel, depth, frames, parts, plan,...  126 us
    pallas_call x1, Pallas kernels, back(): pl.pallas_call(functools.partial(back_kernel, depth, frames, chunk, plan)...  108 us
    pallas_call x1, Pallas kernels, start(): pl.pallas_call(functools.partial(start_kernel, depth), out_shape=(jax.Sha...  33.8 us
    pallas_call x1, Pallas kernels, norm_and_sum(): pl.pallas_call(functools.partial(norm_kernel, depth, images, lats, cols),...  31.9 us
    unnamed x9, local copies, waits for them, and re-layouts  8.61 us

commit v1 on v0

--- a/solution.py
+++ b/solution.py
@@ -27,20 +27,12 @@
 F32 = jnp.float32
 BF16 = jnp.bfloat16
 MESH = pl.DeviceIdType.MESH
-START_PLAN = ("b0", "a1", "c0", "b1", "a2", "c1", "b2", "a3", "c2", "b3", "c3")
+START_PLAN = ('b0', 'a1', 'a2', 'b1', 'c0', 'a3', 'b2', 'c1', 'b3', 'c2', 'c3')
 HEAD_FLIPS = (0,)
 BACK_FLIPS = ()
 HEAD_PLAN = ((2, ('ea1', 'ez2', 'eb0')), (9, ('ez3',)), (12, ('eb1', 'ea2')), (19, ('ec0', 'eb2', 'ea3', 'sz1')), (24, ('ec1', 'eb3', 'sa0')), (26, ('ec2', 'ec3', 'sa1', 'sz2', 'sb0')))
-HEAD_LATE = (
-    ("sz3",),
-    ("sc0", "sb1", "sa2"),
-    (),
-    (),
-    ("sc1", "sb2", "sa3"),
-    ("sc2", "sb3"),
-    ("sc3",),
-)
-BACK_PLAN = ((0, ('a0',)), (1, ('a1',)), (3, ('b0',)), (4, ('a2',)), (7, ('c0', 'b1')), (8, ('a3',)), (11, ('c1', 'b2')), (13, ('c2', 'b3')), (13, ('c3',)))
+HEAD_LATE = (('sz3',), ('sc0', 'sb1', 'sa2'), (), ('sc1',), ('sb2', 'sa3'), ('sc2', 'sb3'), ('sc3',))
+BACK_PLAN = ((0, ('a0',)), (1, ('a1',)), (3, ('b0',)), (4, ('a2',)), (7, ('c0', 'b1')), (8, ('a3',)), (10, ('c1',)), (12, ('b2',)), (13, ('c2', 'b3')), (13, ('c3',)))
 NORM_PLAN = ("a0", "a1", "b0", "a2", "b1", "c0", "a3", "b2", "c1", "b3", "c2", "c3")
 VMEM_LIMIT = 60 * 1024 * 1024
 

time: 319 us -> 311 us (0.975)
  Pallas kernels: 305 us -> 296 us
    pallas_call x1, Pallas kernels: 108 us -> 102 us  [back(): pl.pallas_call(functools.partial(back_kernel, depth, frames, chunk, plan)...]
    pallas_call x1, Pallas kernels: 33.8 us -> 29.5 us  [start(): pl.pallas_call(functools.partial(start_kernel, depth), out_shape=(jax.Sha...]
where the time goes in v1:
time: 311 us; the launch traced here: 310 us
  Pallas kernels  296 us (95%)
  local copies, waits for them, and re-layouts  10.6 us (3%)
    pallas_call x1, Pallas kernels, head(): pl.pallas_call(functools.partial(head_kernel, depth, frames, parts, plan,...  128 us
    pallas_call x1, Pallas kernels, back(): pl.pallas_call(functools.partial(back_kernel, depth, frames, chunk, plan)...  102 us
    pallas_call x1, Pallas kernels, norm_and_sum(): pl.pallas_call(functools.partial(norm_kernel, depth, images, lats, cols),...  32.2 us
    pallas_call x1, Pallas kernels, start(): pl.pallas_call(functools.partial(start_kernel, depth), out_shape=(jax.Sha...  29.5 us
    unnamed x9, local copies, waits for them, and re-layouts  8.61 us

profile of v1, /device:TPU:0, one launch (start us, length us, event | category | flops | bytes accessed | tf_op | source)
XLA Modules:
  0.0 310.2 jit_solution(10925286367970015645)
XLA Ops:
  0.7 0.7 copy.46
  1.5 0.1 reduce
  1.6 0.2 convert_reduce_fusion
  1.8 0.0 copy-start.2
  1.8 0.6 select_reduce_fusion.last
  2.4 0.1 slice_compare_fusion
  2.4 0.6 add_convert_fusion.same
  3.0 0.1 fusion
  3.1 0.5 convert_element_type.8.has
  3.6 29.5 %start.1 = (bf16[32,32,1664]{2,1,0:T(8,128)(2,1)}, bf16[144,1024]{1,0:T(8,128)(2,1)}, bf16[128,1024]{1,0:T(8,128)(2,1)}, f32[8,1024]{1,0:T(8,128)}) custom-call(f32[32,1536]{1,0:T(8,128)} %refs_0_.1, f32[3,32]{1,0:T(4,128)} %bitcast.30, f32[3,32]{1,0:T(4,128)} %bitcast.32, f32[32,4096]{1,0:T(8,128)} %refs_2_.1, f32[128,1024]{1,0:T(8,128)} %refs_3_.1, ...), custom_call_target="tpu_custom_call" | custom-call | tf_op jit(solution)/shard_map/start/pallas_call | solution.py:497
  33.2 0.0 copy-done.2
  33.2 128.0 %head.1 = (bf16[3072,512]{1,0:T(8,128)(2,1)}, bf16[3072,512]{1,0:T(8,128)(2,1)}, bf16[4,24,16,512]{3,2,1,0:T(8,128)(2,1)}, bf16[24,16,512]{2,1,0:T(8,128)(2,1)},...) custom-call(s32[12]{0:T(128)} %copy-done.2, ...), custom_call_target="tpu_custom_call" | custom-call | tf_op jit(solution)/shard_map/head/pallas_call | solution.py:1902
  161.2 101.8 %back.1 = (bf16[3072,1024]{1,0:T(8,128)(2,1)}, f32[384,1024]{1,0:T(8,128)}, bf16[1024,1664]{1,0:T(8,128)(2,1)}, f32[272,1024]{1,0:T(8,128)}) custom-call(s32[12]{0:T(128)} %copy-done.2, s32[24]{0:T(128)} %select_reduce_fusion.last, s32[24]{0:T(128)} %convert_element_type.8.has, s32[12]{0:T(128)} %add_convert_fusion.same, ...), custom_call_target="tpu_custom_call" | custom-call | tf_op jit(solution)/shard_map/back/pallas_call | solution.py:1366
  262.9 32.2 %norm.1 = (f32[8,128]{1,0:T(8,128)}, f32[32,1664]{1,0:T(8,128)}) custom-call(bf16[32,32,1664]{2,1,0:T(8,128)(2,1)} %bitcast.25, f32[272,1024]{1,0:T(8,128)} %get-tuple-element.80.feed_ref), custom_call_target="tpu_custom_call" | custom-call | tf_op jit(solution)/shard_map/norm/pallas_call | solution.py:2009
  295.1 0.0 copy-start
  295.1 4.9 %update.1 = (f32[8,128]{1,0:T(8,128)}, f32[32,1536]{1,0:T(8,128)}, f32[16,1024]{1,0:T(8,128)}, f32[32,4096]{1,0:T(8,128)}, f32[128,1024]{1,0:T(8,128)}, /*index=...) custom-call(f32[8,128]{1,0:T(8,128)} %get-tuple-element.81.norm_ref,, ...), custom_call_target="tpu_custom_call" | custom-call | tf_op jit(solution)/shard_map/update/pallas_call | solution.py:2084
  300.1 1.2 slice.11
  301.3 0.0 copy-done
  301.3 1.1 copy.50
  302.4 0.0 copy-start.1
  302.4 6.3 %copy.51 = bf16[3072,1024]{1,0:T(8,128)(2,1)} copy(bf16[3072,1024]{1,0:T(8,128)(2,1)} %get-tuple-element.125) | data formatting | bytes 12582912
  308.7 0.0 copy-done.1
  308.7 1.1 copy.52
  (3 shorter events, 0.1 us)
Async XLA Ops:
  1.8 31.4 %copy-start.2 = (s32[12]{0:T(128)}, s32[12]{0:T(128)S(1)}, u32[]{:S(2)}) copy-start(s32[12]{0:T(128)S(1)} %broadcast_clamp_fusion.ids) | copy-start | bytes 148
  295.1 6.2 %copy-start = (f32[384,1024]{1,0:T(8,128)S(1)}, f32[384,1024]{1,0:T(8,128)}, u32[]{:S(2)}) copy-start(f32[384,1024]{1,0:T(8,128)} %get-tuple-element.66) | copy-start | bytes 4718596
  302.4 6.3 %copy-start.1 = (f32[384,1024]{1,0:T(8,128)S(1)}, f32[384,1024]{1,0:T(8,128)}, u32[]{:S(2)}) copy-start(f32[384,1024]{1,0:T(8,128)} %get-tuple-element.78) | copy-start | bytes 4718596
